TPU v7x, 256 devices: a whole 4x4x8 slice. The times are simulated.
256 devices in a mesh: ctx: 8 (over x, core), fsdp: 32 (over y, z).
Axes of the slice: x: 4, y: 4, z: 8, core: 2. Of those that a mesh axis runs over, the one named last changes fastest.
Arguments:
- tokens: bfloat16 [65536, 2560], P(('ctx', 'fsdp')), may hold values from -6 to 6
- w_in: bfloat16 [2560, 4352], P('fsdp'), may hold values from -0.125 to 0.125
- conv_weight: float32 [4, 4352], replicated, may hold values from -3 to 3
- log_decay: float32 [65536, 64], P('ctx', 'fsdp'), may hold values from -2 to 0, as said below
- norm_gain: float32 [4096], P('fsdp'), may hold values from 0.1 to 1.9
Outputs:
- layer_out: bfloat16 [65536, 4096], P('ctx', 'fsdp')
Inputs may be any that keep to these rules, and one draw needn't show every extreme that they name: `log_decay`: log of a per-position, per-head decay.
All inputs are finite; a program needn't handle non-finite values.
Results may differ from a plain program's by a relative error of at most 0.0037.
Values may be sent and summed in bfloat16 or wider, within the bound.
A program may use at most 128 MiB of HBM per device.

v0:
```python
import math

import jax
import jax.numpy as jnp
from jax import lax
from jax.sharding import PartitionSpec as P

H = 64
P_SIZE = 64
N = 128
Q = 256


epsilon = 1e-05


def shifted(block, axis, distance):
    devices = range(lax.axis_size(axis))
    route = [(i - distance, i) for i in devices if i - distance in devices]
    return lax.ppermute(block, axis, route)


def carried_in(array, axis, combine, identity):
    length, index = (lax.axis_size(axis), lax.axis_index(axis))
    everything = jax.tree.map(
        lambda part, kind: lax.all_gather(part.astype(kind), axis),
        array,
        (jnp.bfloat16, jnp.bfloat16),
    )
    start = jax.tree.map(
        lambda part, zero: jnp.broadcast_to(jnp.asarray(zero, part.dtype), part.shape),
        array,
        identity,
    )

    def lap(k, before):
        reached = k < index
        new = combine(
            before, jax.tree.map(lambda part, own: part[k].astype(own.dtype), everything, array)
        )
        return jax.tree.map(lambda a, b: jnp.where(reached, a, b), new, before)

    return lax.fori_loop(0, length, lap, start)


def combine_carry(earlier, later):
    return (earlier[0] * later[0], later[0][..., None, None] * earlier[1] + later[1])


def body(tokens, w_in, conv_weight, log_decay, norm_gain):
    tok_rows = tokens.shape[0]
    kernel = conv_weight.shape[0]
    columns = w_in.shape[1]
    projected = jnp.dot(
        tokens, lax.all_gather(w_in, "fsdp", axis=0, tiled=True), preferred_element_type=jnp.float32
    ).astype(jnp.bfloat16)
    rim_rows = shifted(projected[tok_rows - (kernel - 1) :], ("ctx", "fsdp"), 1)
    extended = jnp.concatenate([rim_rows, projected], axis=0)
    summed = jnp.zeros((tok_rows, columns), jnp.float32)
    for offset in range(kernel):
        summed = summed + conv_weight[offset] * extended[offset : offset + tok_rows].astype(
            jnp.float32
        )
    conv_out = jax.nn.silu(summed).astype(jnp.bfloat16)
    inner_rows = lax.all_to_all(
        conv_out[:, : H * P_SIZE], "fsdp", split_axis=1, concat_axis=0, tiled=True
    )
    state_rows = lax.all_gather(conv_out[:, H * P_SIZE :], "fsdp", axis=0, tiled=True)
    ctx_rows = inner_rows.shape[0]
    heads_dev = log_decay.shape[1]
    blocks = ctx_rows // Q
    inner_blocks = inner_rows.reshape(blocks, Q, heads_dev, P_SIZE)
    b_blocks = state_rows[:, :N].reshape(blocks, Q, N)
    c_blocks = state_rows[:, N:].reshape(blocks, Q, N)
    cumulative = jnp.cumsum(log_decay.reshape(blocks, Q, heads_dev), axis=1)
    totals = cumulative[:, -1, :]
    end_weights = jnp.exp(totals[:, None, :] - cumulative)
    scaled_inner = (inner_blocks.astype(jnp.float32) * end_weights[:, :, :, None]).astype(
        jnp.bfloat16
    )
    contribution = jnp.einsum(
        "bshp,bsn->bhpn", scaled_inner, b_blocks, preferred_element_type=jnp.float32
    )
    block_products, running_state = lax.associative_scan(
        combine_carry, (jnp.exp(totals), contribution), axis=0
    )
    zero_state = jnp.zeros((1, heads_dev, P_SIZE, N), jnp.float32)
    local_starts = jnp.concatenate([zero_state, running_state[:-1]], axis=0)
    finals = running_state[-1]
    block_decay = jnp.exp(jnp.sum(totals, axis=0))
    offsets = jnp.cumsum(totals, axis=0) - totals
    lower_mask = jnp.arange(Q)[:, None] >= jnp.arange(Q)[None, :]
    per_group = math.gcd(blocks, max(1, 2048 // Q))
    rounds = blocks // per_group

    def grouped(values):
        return values.reshape((rounds, per_group) + values.shape[1:])

    def group_outputs(pieces):
        inner_part, b_part, c_part, cum_part, start_part = pieces
        scores = jnp.einsum("gtn,gsn->gts", c_part, b_part, preferred_element_type=jnp.float32)
        cum_heads = cum_part.transpose(0, 2, 1)
        differences = cum_heads[:, :, :, None] - cum_heads[:, :, None, :]
        decay_weights = jnp.where(
            lower_mask[None, None], jnp.exp(jnp.minimum(differences, 0.0)), 0.0
        )
        weighted = (scores[:, None] * decay_weights).astype(jnp.bfloat16)
        within = jnp.einsum(
            "ghts,gshp->gthp", weighted, inner_part, preferred_element_type=jnp.float32
        )
        from_state = jnp.exp(cum_part)[..., None] * jnp.einsum(
            "gtn,ghpn->gthp",
            c_part.astype(jnp.float32),
            start_part,
            precision=lax.Precision.HIGHEST,
        )
        return within + from_state

    mapped = lax.map(
        group_outputs,
        (
            grouped(inner_blocks),
            grouped(b_blocks),
            grouped(c_blocks),
            grouped(cumulative),
            grouped(local_starts),
        ),
    )
    outputs = mapped.reshape(blocks, Q, heads_dev, P_SIZE)
    identity = (jnp.ones((heads_dev,), jnp.float32), jnp.zeros((heads_dev, P_SIZE, N), jnp.float32))
    carry_decay, carried = carried_in((block_decay, finals), "ctx", combine_carry, identity)
    correction = jnp.exp(cumulative + offsets[:, None, :])[..., None] * jnp.einsum(
        "btn,hpn->bthp", c_blocks.astype(jnp.float32), carried, precision=lax.Precision.HIGHEST
    )
    outputs = outputs + correction
    mean_square = jnp.mean(outputs * outputs, axis=-1, keepdims=True)
    normed = outputs * lax.rsqrt(mean_square + epsilon) * norm_gain.reshape(heads_dev, P_SIZE)
    return normed.reshape(ctx_rows, heads_dev * P_SIZE).astype(jnp.bfloat16)


def solution(mesh):
    placed = (P(("ctx", "fsdp"), None), P("fsdp", None), P(), P("ctx", "fsdp"), P("fsdp"))
    return jax.shard_map(
        body, mesh=mesh, in_specs=placed, out_specs=P("ctx", "fsdp"), check_vma=False
    )
```

profile of v0, /device:TPU:1, one launch (start us, length us, event | category | flops | bytes accessed | tf_op | source)
XLA Modules:
  0.0 449.4 jit_solution(13795887536512870053)
XLA Ops:
  6.5 0.7 all-gather.4.cloned.1.call-update
  7.3 174.4 %all-gather.4.cloned.1.call-done = bf16[2560,4352]{1,0:T(8,128)(2,1)} async-done(((bf16[80,4352]{1,0:T(8,128)(2,1)}), bf16[2560,4352]{1,0:T(8,128)(2,1)}) %all-gather.4.cloned.1.call-update) | async-done | bytes 22282256 | tf_op jit(solution)/shard_map/all_gather | solution.py:55
  181.7 10.7 %convolution_convert_fusion = bf16[256,4352]{1,0:T(8,128)(2,1)S(1)} fusion(bf16[256,2560]{1,0:T(8,128)(2,1)S(1)} %copy-done, bf16[2560,4352]{1,0:T(8,128)(2,1)} %all-gather.4.cloned.1.call-done), kind=kOutput, calls=%fused_computation.35 | convolution fusion | flops 5705367552 | bytes 25821184 | tf_op jit(solution)/shard_map/dot_general | solution.py:54
  192.4 1.9 collective-permute-start
  194.6 6.4 %collective-permute-done = bf16[3,4352]{1,0:T(4,128)(2,1)S(1)} collective-permute-done((bf16[3,4352]{1,0:T(4,128)(2,1)S(1)}, bf16[3,4352]{1,0:T(4,128)(2,1)S(1)}, u32[]{:S(2)}, u32[]{:S(2)}) %collective-permute-start) | collective-permute-done | bytes 26144 | tf_op jit(solution)/shard_map/ppermute | solution.py:20
  201.0 3.0 multiply_convert_fusion.4
  204.7 1.9 copy_bitcast_fusion.1
  206.7 4.1 all-to-all-start
  210.8 1.2 reduce-window.6
  212.2 0.7 bitcast_bitcast_fusion.2
  215.5 14.0 %all-reduce.11 = bf16[16]{0:T(256)(128)(2,1)S(1)} all-reduce(bf16[16]{0:T(256)(128)(2,1)S(1)} %dynamic-update-slice), channel_id=2, replica_groups=mesh['ctx'=8,'fsdp'=32] {'ctx'}, use_global_device_ids=true, to_apply=%add.11 | all-reduce | flops 16 | bytes 64
  230.8 0.7 reshape.108
  233.4 0.8 slice_reduce_fusion.5
  234.4 30.5 %all-to-all-done = bf16[256,32,128]{2,0,1:T(8,128)(2,1)S(1)} async-done(((bf16[256,32,128]{2,0,1:T(8,128)(2,1)}), bf16[256,32,128]{2,0,1:T(8,128)(2,1)S(1)}, u32[]{:S(2)}, u32[]{:S(2)}) %all-to-all-start) | async-done | bytes 2097184 | tf_op jit(solution)/shard_map/all_to_all | solution.py:65
  264.9 2.9 copy.115
  267.7 19.8 %all-gather.6.cloned.1.call-done = bf16[8192,256]{1,0:T(8,128)(2,1)} async-done(((bf16[256,256]{1,0:T(8,128)(2,1)}), bf16[8192,256]{1,0:T(8,128)(2,1)}) %all-gather.6.cloned.1.call-update) | async-done | bytes 4194320 | tf_op jit(solution)/shard_map/all_gather | solution.py:68
  287.5 2.6 fusion.41
  290.4 0.7 fusion.31
  292.9 0.9 copy-done.5
  294.1 1.9 pad.34
  296.1 1.9 pad.35
  298.0 1.8 add.147
  299.8 5.1 %pad.37 = f32[8,2,64,128]{3,2,1,0:T(8,128)} pad(f32[4,2,64,128]{3,2,1,0:T(8,128)} %add.147, f32[]{:T(128)} %constant.62.clone.1), padding=1_0_1x0_0_0x0_0_0x0_0_0 | pad | bytes 786436 | tf_op jit(solution)/shard_map/pad | solution.py:84
  304.9 1.2 fusion.36
  306.1 0.7 pad_maximum_fusion.3
  306.9 5.1 %pad.36 = f32[8,2,64,128]{3,2,1,0:T(8,128)} pad(f32[4,2,64,128]{3,2,1,0:T(8,128)} %pad_maximum_fusion.3, f32[]{:T(128)} %constant.62.clone.1), padding=0_1_1x0_0_0x0_0_0x0_0_0 | pad | bytes 786436 | tf_op jit(solution)/shard_map/pad | solution.py:84
  312.0 2.1 add.149
  314.1 1.3 fusion.35
  315.5 5.9 %pad.38 = f32[16,2,64,128]{3,2,1,0:T(8,128)} pad(f32[8,2,64,128]{3,2,1,0:T(8,128)S(1)} %pad_maximum_fusion.2, f32[]{:T(128)} %constant.62.clone.1), padding=0_1_1x0_0_0x0_0_0x0_0_0 | pad | bytes 1572868 | tf_op jit(solution)/shard_map/pad | solution.py:84
  321.4 5.8 %pad.39 = f32[16,2,64,128]{3,2,1,0:T(8,128)} pad(f32[8,2,64,128]{3,2,1,0:T(8,128)S(1)} %copy-done.6, f32[]{:T(128)} %constant.62.clone.1), padding=1_0_1x0_0_0x0_0_0x0_0_0 | pad | bytes 1572868 | tf_op jit(solution)/shard_map/pad | solution.py:84
  327.2 1.7 add.151
  328.9 11.0 %pad.93 = f32[31,2,64,128]{3,2,1,0:T(8,128)} pad(f32[16,2,64,128]{3,2,1,0:T(8,128)S(1)} %add.151, f32[]{:T(128)} %constant.62.clone.1), padding=0_0_1x0_0_0x0_0_0x0_0_0 | pad | bytes 3080196
  339.9 11.1 %pad.41 = f32[32,2,64,128]{3,2,1,0:T(8,128)} pad(f32[16,2,64,128]{3,2,1,0:T(8,128)S(1)} %add.151, f32[]{:T(128)} %constant.62.clone.1), padding=1_0_1x0_0_0x0_0_0x0_0_0 | pad | bytes 3145732 | tf_op jit(solution)/shard_map/pad | solution.py:84
  351.0 0.8 add_convert_fusion
  351.8 16.9 %all_gather.17 = bf16[8,2,64,128]{3,2,1,0:T(8,128)(2,1)S(1)} all-gather(bf16[1,2,64,128]{3,2,1,0:T(8,128)(2,1)S(1)} %add_convert_fusion), channel_id=1, replica_groups=mesh['ctx'=8,'fsdp'=32] {'ctx'}, dimensions={0}, use_global_device_ids=true | all-gather | bytes 294912 | tf_op jit(solution)/shard_map/all_gather | solution.py:26
  368.7 6.1 %while.26 = (s32[]{:T(128)}, f32[2,64,128]{2,1,0:T(8,128)S(1)}, s32[]{:T(128)}, bf16[8,2]{1,0:T(8,128)(2,1)}, bf16[8,2,64,128]{3,2,1,0:T(8,128)(2,1)S(1)}, /*index=5*/s32[]{:T(128)}, s32[]{:T(128)}) while((s32[]{:T(128)}, f32[2,64,128]{2,1,0:T(8,128)S(1)}, s32[]{:T(128)}, bf16[8,2]{1,0:T(8,128)(2,1)}, ...), condition=%wide.region_7.8_spmd.clone, body=%wide.region_6.7_spmd.clone.sunk | while | flops 81926 | bytes 163973 | solution.py:43
  368.7 0.7 bitcast_convert_fusion.2
  369.5 0.7 bitcast_convert_fusion.2
  371.8 0.7 bitcast_convert_fusion.2
  374.8 2.0 fusion.34
  376.9 11.1 %pad.40 = f32[32,2,64,128]{3,2,1,0:T(8,128)} pad(f32[16,2,64,128]{3,2,1,0:T(8,128)S(1)} %pad_maximum_fusion.1, f32[]{:T(128)} %constant.62.clone.1), padding=0_1_1x0_0_0x0_0_0x0_0_0 | pad | bytes 3145732 | tf_op jit(solution)/shard_map/pad | solution.py:84
  387.9 2.6 slice_add_fusion
  390.5 1.5 concatenate.23
  392.0 29.5 %while.25 = (s32[]{:T(128)}, f32[4,8,256,2,64]{2,4,3,1,0:T(8,128)}, bf16[4,8,256,2,64]{2,4,3,1,0:T(8,128)(2,1)}, bf16[4,8,256,128]{3,2,1,0:T(8,128)(2,1)S(1)}, b...) while((s32[]{:T(128)}, f32[4,8,256,2,64]{2,4,3,1,0:T(8,128)}, ...), condition=%wide.region_3.4_spmd.clone, body=%wide.region_2.3_spmd.clone.sunk | while | flops 676921344 | bytes 10242661 | solution.py:119
  392.0 0.8 constant_dynamic-slice_fusion.2
  392.7 1.5 fusion.64
  394.3 2.4 fusion.65
  396.7 2.6 fusion.66
  399.4 0.7 constant_dynamic-slice_fusion.2
  400.1 1.5 fusion.64
  401.6 2.4 fusion.65
  404.1 2.7 fusion.66
  406.8 0.7 constant_dynamic-slice_fusion.2
  407.5 1.5 fusion.64
  409.0 2.4 fusion.65
  411.5 2.6 fusion.66
  414.2 0.7 constant_dynamic-slice_fusion.2
  414.9 1.5 fusion.64
  416.4 2.4 fusion.65
  418.9 2.6 fusion.66
  421.5 4.6 %multiply_reduce_fusion = (f32[32,256,2]{1,2,0:T(2,128)S(1)}, f32[32,256,2,64]{1,3,2,0:T(8,128)S(1)}) fusion(bf16[32,256,128,1]{2,1,3,0:T(8,128)(2,1)S(1)} %bitcast.128, f32[2,64,128]{2,1,0:T(8,128)S(1)} %get-tuple-element.142, f32[32,256,2]{1,2,0:T(2,128)S(1)} %copy-done.7, f32[4,8,256,2,64]{2,4,3,1,0:T(8,128)} %get-tuple-element.141), kind=kOutput, calls=%fused_computation.41 | convolution fusion | flops 1614790656 | bytes 10682368 | tf_op jit(solution)/shard_map/btn,hpn->bthp/dot_general | solution.py:132
  426.2 0.8 multiply_convert_fusion.5
  427.0 7.8 %copy.137 = bf16[32,256,2,64]{3,2,1,0:T(2,128)(2,1)} copy(bf16[32,256,2,64]{1,3,2,0:T(8,128)(2,1)S(1)} %multiply_convert_fusion.5) | data formatting | bytes 4194304 | tf_op jit(solution)/shard_map/convert_element_type | solution.py:138
  434.8 7.8 %reshape.120 = bf16[8192,128]{1,0:T(8,128)(2,1)} reshape(bf16[32,256,2,64]{3,2,1,0:T(2,128)(2,1)} %copy.137) | data formatting | bytes 4194304 | tf_op jit(solution)/shard_map/convert_element_type | solution.py:138
  (121 shorter events, 13.2 us)
Async XLA Ops:
  6.5 175.2 %copy-start = (bf16[256,2560]{1,0:T(8,128)(2,1)S(1)}, bf16[256,2560]{1,0:T(8,128)(2,1)}, u32[]{:S(2)}) copy-start(bf16[256,2560]{1,0:T(8,128)(2,1)} %param.9) | copy-start | bytes 3932164
  6.5 175.2 %all-gather.4.cloned.1.call-start = ((), (), s32[]{:S(2)}) async-start(), calls=%async_computation.1 | async-start | bytes 22978560 | tf_op jit(solution)/shard_map/all_gather | solution.py:55
  7.3 187.1 %copy-start.9 = (f32[4,4352]{1,0:T(4,128)S(1)}, f32[4,4352]{1,0:T(4,128)}, u32[]{:S(2)}) copy-start(f32[4,4352]{1,0:T(4,128)} %param.11) | copy-start | bytes 208900
  7.3 280.3 %all-gather.6.cloned.1.call-start = ((), (), s32[]{:S(2)}) async-start(), calls=%async_computation.2 | async-start | bytes 4325376 | tf_op jit(solution)/shard_map/all_gather | solution.py:68
  192.4 8.6 %collective-permute-start = (bf16[3,4352]{1,0:T(4,128)(2,1)S(1)}, bf16[3,4352]{1,0:T(4,128)(2,1)S(1)}, u32[]{:S(2)}, u32[]{:S(2)}) collective-permute-start(bf16[3,4352]{1,0:T(4,128)(2,1)S(1)} %slice.215), channel_id=1, source_target_pairs={{0,1},{1,2},{2,3},{3,4},{4,5},{5,6},{6,7},{7,8},{8,9},{9,10},{10,1... | collective-permute-start | bytes 78344 | tf_op jit(solution)/shard_map/ppermute | solution.py:20
  206.6 4.2 copy-start.10
  206.6 7.0 %copy-start.14 = (u32[256]{0:T(256)S(1)}, u32[256]{0:T(256)}, u32[]{:S(2)}) copy-start(u32[256]{0:T(256)} %constant.94) | copy-start | bytes 3076
  206.7 26.1 %copy-start.13 = (f32[128]{0:T(128)S(1)}, f32[128]{0:T(128)}, u32[]{:S(2)}) copy-start(f32[128]{0:T(128)} %param.13) | copy-start | bytes 1540
  206.7 58.2 %all-to-all-start = ((bf16[256,32,128]{2,0,1:T(8,128)(2,1)}), bf16[256,32,128]{2,0,1:T(8,128)(2,1)S(1)}, u32[]{:S(2)}, u32[]{:S(2)}) async-start(bf16[256,32,128]{2,0,1:T(8,128)(2,1)} %copy_bitcast_fusion.1), calls=%async_computation | async-start | bytes 4194304 | tf_op jit(solution)/shard_map/all_to_all | solution.py:65
  287.5 2.9 copy-start.4
  290.2 1.3 copy-start.2
  291.5 1.4 copy-start.3
  291.7 2.3 copy-start.12
  292.9 0.9 copy-start.5
  293.8 12.3 %slice-start.1 = ((f32[8,2,64,128]{3,2,1,0:T(8,128)}), f32[1,2,64,128]{3,2,1,0:T(8,128)S(1)}, s32[]{:S(2)}) async-start(f32[8,2,64,128]{3,2,1,0:T(8,128)} %copy-done.5), calls=%async_computation.4 | async-start | bytes 131072 | tf_op jit(solution)/shard_map/slice | solution.py:84
  306.1 9.3 %copy-start.8 = (f32[1,2,64,128]{3,2,1,0:T(8,128)S(1)}, f32[1,2,64,128]{3,2,1,0:T(8,128)}, u32[]{:S(2)}) copy-start(f32[1,2,64,128]{3,2,1,0:T(8,128)} %slice.228) | copy-start | bytes 196612
  315.4 6.0 %copy-start.6 = (f32[8,2,64,128]{3,2,1,0:T(8,128)S(1)}, f32[8,2,64,128]{3,2,1,0:T(8,128)}, u32[]{:S(2)}) copy-start(f32[8,2,64,128]{3,2,1,0:T(8,128)} %add.149) | copy-start | bytes 1572868
  368.7 8.1 %slice-start = ((f32[32,2,64,128]{3,2,1,0:T(8,128)}), f32[1,2,64,128]{3,2,1,0:T(8,128)S(1)}, s32[]{:S(2)}) async-start(f32[32,2,64,128]{3,2,1,0:T(8,128)} %copy-done.3), calls=%async_computation.3 | async-start | bytes 131072 | tf_op jit(solution)/shard_map/slice | solution.py:84
  392.0 29.5 %copy-start.7 = (f32[32,256,2]{1,2,0:T(2,128)S(1)}, f32[32,256,2]{1,2,0:T(2,128)}, u32[]{:S(2)}) copy-start(f32[32,256,2]{1,2,0:T(2,128)} %copy.131) | copy-start | bytes 196612
  421.5 4.7 %copy-start.11 = (f32[2,64]{1,0:T(2,128)S(1)}, f32[2,64]{1,0:T(2,128)}, u32[]{:S(2)}) copy-start(f32[2,64]{1,0:T(2,128)} %mul.251) | copy-start | bytes 1540
  427.0 15.6 %copy-start.1 = (bf16[256,2560]{1,0:T(8,128)(2,1)S(1)}, bf16[256,2560]{1,0:T(8,128)(2,1)}, u32[]{:S(2)}) copy-start(bf16[256,2560]{1,0:T(8,128)(2,1)} %param.9) | copy-start | bytes 3932164
Sparse Core Ops, SparseCore 0:
  9.9 171.7 all-gather.3
  204.9 82.6 all-gather.5
where the time goes:
time: 452 us; the launch traced here: 449 us
  waiting for transfers between devices  232 us (51%)
  local copies, waits for them, and re-layouts  96.5 us (21%)
  matrix products  42.2 us (9%)
  blocking collectives  30.9 us (7%)
  other arithmetic  27.3 us (6%)
  between operations  14.5 us (3%)
  starting transfers between devices  6.11 us (1%)
    all_gather x1, waiting for transfers between devices, body(): lax.all_gather(w_in, 'fsdp', axis=0, tiled=True)  174 us
    pad x8, local copies, waits for them, and re-layouts, body(): lax.associative_scan(combine_carry, (jnp.exp(totals), contribution), axis=0)  48 us
    all_to_all x1, waiting for transfers between devices, body(): lax.all_to_all(conv_out[:, :H * P_SIZE], 'fsdp', split_axis=1, concat_axi...  30.5 us
    all_gather x1, waiting for transfers between devices, body(): lax.all_gather(conv_out[:, H * P_SIZE:], 'fsdp', axis=0, tiled=True)  19.8 us
    all_gather x1, blocking collectives, carried_in(): lax.all_gather(part.astype(kind), axis)  16.9 us
    convert_element_type x2, local copies, waits for them, and re-layouts, body(): return normed.reshape(ctx_rows, heads_dev * P_SIZE).astype(jnp.bfloat16)  15.6 us
    unnamed x1, blocking collectives  14 us
    unnamed x34, local copies, waits for them, and re-layouts  13.8 us
  transfers between devices with their start and end apart: 4, of which 4 were waited for; matrix products, arithmetic and copies ran while one was open for 3% of the time, Pallas kernels for 0%

commit v1 on v0

v1 whole, which is shorter than its diff:
```python
import functools

import jax
import jax.numpy as jnp
from jax import lax
from jax.experimental import pallas as pl
from jax.experimental.pallas import tpu as pltpu
from jax.sharding import PartitionSpec as P

H = 64
P_SIZE = 64
N = 128
Q = 256
HALO = 16
MESH = pl.DeviceIdType.MESH
F32 = jnp.float32
BF16 = jnp.bfloat16
epsilon = 1e-05

NT = (((1,), (1,)), ((), ()))
TN = (((0,), (0,)), ((), ()))


def split2(v):
    high = v.astype(BF16)
    low = (v - high.astype(F32)).astype(BF16)
    return high, low


def lane_of(shape):
    return lax.broadcasted_iota(jnp.int32, shape, 1)


def scan_kernel(
    n_ctx,
    blocks,
    proj,
    bc,
    decay,
    taps,
    gain,
    out,
    cum,
    inner,
    starts,
    offsets,
    within,
    halo,
    mine,
    carries,
    halo_sems,
    send_sems,
    recv_sems,
):
    me = lax.axis_index("ctx")
    barrier = pltpu.get_barrier_semaphore()
    for r in range(1, n_ctx):
        pl.semaphore_signal(
            barrier,
            inc=1,
            device_id={"ctx": lax.rem(me + r, n_ctx)},
            device_id_type=MESH,
        )

    upper = (
        lax.broadcasted_iota(jnp.int32, (Q, Q), 0)
        <= lax.broadcasted_iota(jnp.int32, (Q, Q), 1)
    ).astype(BF16)
    steps = decay[...].reshape(blocks * 8, Q)
    high, rest = split2(steps)
    lowest = (steps - high.astype(F32) - rest.astype(F32)).astype(BF16)
    total = jnp.dot(lowest, upper, preferred_element_type=F32)
    total = total + jnp.dot(rest, upper, preferred_element_type=F32)
    total = total + jnp.dot(high, upper, preferred_element_type=F32)
    cum[...] = total.reshape(blocks, 8, Q)

    pl.semaphore_wait(barrier, n_ctx - 1)
    rows = blocks * Q
    halo_copy = pltpu.make_async_remote_copy(
        src_ref=proj.at[pl.ds(rows - HALO, HALO)],
        dst_ref=halo,
        send_sem=halo_sems.at[0],
        recv_sem=halo_sems.at[1],
        device_id={"ctx": lax.rem(me + 1, n_ctx)},
        device_id_type=MESH,
    )
    halo_copy.start()
    halo_copy.wait()

    def by_position(block):
        rows_of = cum[block]
        both = jnp.concatenate(
            [
                jnp.broadcast_to(rows_of[h : h + 1], (P_SIZE, Q))
                for h in range(2)
            ],
            axis=0,
        )
        return both.T

    def states(block, carry):
        tail, state, offset = carry
        base = pl.multiple_of(block * Q, Q)
        current = proj[pl.ds(base, Q), :].astype(F32)
        window = jnp.concatenate([tail, current], axis=0)
        summed = taps[0:1] * window[5 : 5 + Q]
        for k in range(1, 4):
            summed = summed + taps[k : k + 1] * window[5 + k : 5 + k + Q]
        own = jax.nn.silu(summed).astype(BF16)
        inner[pl.ds(base, Q), :] = own
        positions = by_position(block)
        last = positions[Q - 1 : Q]
        scaled = (own.astype(F32) * jnp.exp(last - positions)).astype(BF16)
        b_part = bc[pl.ds(base, Q), :N]
        added = lax.dot_general(b_part, scaled, TN, preferred_element_type=F32)
        starts[block] = state
        offsets[block] = jnp.broadcast_to(offset, (8, N))
        return current[Q - 8 :], jnp.exp(last) * state + added, offset + last

    first = jnp.where(me == 0, 0.0, halo[...].astype(F32))[HALO - 8 :]
    _, state, offset = lax.fori_loop(
        0,
        blocks,
        states,
        (first, jnp.zeros((N, 2 * P_SIZE), F32), jnp.zeros((1, 2 * P_SIZE), F32)),
    )
    mine[0:N] = state
    mine[N : N + 8] = jnp.broadcast_to(jnp.exp(offset), (8, 2 * P_SIZE))

    def carry_copy(r):
        return pltpu.make_async_remote_copy(
            src_ref=mine,
            dst_ref=carries.at[r - 1],
            send_sem=send_sems.at[r - 1],
            recv_sem=recv_sems.at[r - 1],
            device_id={"ctx": lax.rem(me + r, n_ctx)},
            device_id_type=MESH,
        )

    for r in range(1, n_ctx):
        carry_copy(r).start()

    mask = lax.broadcasted_iota(jnp.int32, (Q, Q), 0) >= lax.broadcasted_iota(
        jnp.int32, (Q, Q), 1
    )
    first_head = lane_of((Q, 2 * P_SIZE)) < P_SIZE

    def inside(block, _):
        base = pl.multiple_of(block * Q, Q)
        b_part = bc[pl.ds(base, Q), :N]
        c_part = bc[pl.ds(base, Q), N:]
        own = inner[pl.ds(base, Q), :]
        scores = lax.dot_general(c_part, b_part, NT, preferred_element_type=F32)
        rows_of = cum[block]
        parts = []
        for h in range(2):
            along = rows_of[h : h + 1]
            down = jnp.broadcast_to(along, (2 * P_SIZE, Q)).T
            down = jnp.concatenate([down, down], axis=1)
            weights = jnp.exp(jnp.where(mask, down - along, -1e30))
            weighted = (scores * weights).astype(BF16)
            parts.append(jnp.dot(weighted, own, preferred_element_type=F32))
        within[pl.ds(base, Q), :] = jnp.where(first_head, parts[0], parts[1])
        return 0

    lax.fori_loop(0, blocks, inside, 0)

    for r in range(1, n_ctx):
        carry_copy(r).wait()
    carried = jnp.zeros((N, 2 * P_SIZE), F32)
    for r in range(n_ctx - 1, 0, -1):
        new = carries[r - 1, N : N + 1] * carried + carries[r - 1, 0:N]
        carried = jnp.where(me - r >= 0, new, carried)

    same_head = (
        lax.broadcasted_iota(jnp.int32, (2 * N, 2 * P_SIZE), 0) % (2 * P_SIZE)
        // P_SIZE
        == lane_of((2 * N, 2 * P_SIZE)) // P_SIZE
    )
    averaging = jnp.where(same_head, 1.0 / P_SIZE, 0.0).astype(BF16)

    def finish(block, _):
        base = pl.multiple_of(block * Q, Q)
        c_part = bc[pl.ds(base, Q), N:]
        state = starts[block] + jnp.exp(offsets[block, 0:1]) * carried
        from_state = jnp.dot(
            jnp.concatenate([c_part, c_part], axis=1),
            jnp.concatenate(split2(state), axis=0),
            preferred_element_type=F32,
        )
        value = within[pl.ds(base, Q), :] + jnp.exp(by_position(block)) * from_state
        squares = jnp.concatenate(split2(value * value), axis=1)
        mean = jnp.dot(squares, averaging, preferred_element_type=F32)
        normed = value * lax.rsqrt(mean + epsilon) * gain[0:1]
        out[pl.ds(base, Q), :] = normed.astype(BF16)
        return 0

    lax.fori_loop(0, blocks, finish, 0)


def scan(n_ctx, proj, bc, decay, taps, gain):
    rows = proj.shape[0]
    blocks = rows // Q
    width = 2 * P_SIZE
    vmem = pl.BlockSpec(memory_space=pltpu.VMEM)
    return pl.pallas_call(
        functools.partial(scan_kernel, n_ctx, blocks),
        out_shape=jax.ShapeDtypeStruct((rows, width), BF16),
        in_specs=[vmem] * 5,
        out_specs=vmem,
        scratch_shapes=[
            pltpu.VMEM((blocks, 8, Q), F32),
            pltpu.VMEM((rows, width), BF16),
            pltpu.VMEM((blocks, N, width), F32),
            pltpu.VMEM((blocks, 8, width), F32),
            pltpu.VMEM((rows, width), F32),
            pltpu.VMEM((HALO, width), BF16),
            pltpu.VMEM((N + 8, width), F32),
            pltpu.VMEM((n_ctx - 1, N + 8, width), F32),
            pltpu.SemaphoreType.DMA((2,)),
            pltpu.SemaphoreType.DMA((n_ctx - 1,)),
            pltpu.SemaphoreType.DMA((n_ctx - 1,)),
        ],
        compiler_params=pltpu.CompilerParams(
            collective_id=1, has_side_effects=True, vmem_limit_bytes=48 * 2**20
        ),
    )(proj, bc, decay, taps, gain)


def shifted(block, axis, distance):
    devices = range(lax.axis_size(axis))
    route = [(i - distance, i) for i in devices if i - distance in devices]
    return lax.ppermute(block, axis, route)


def scan_operands(log_decay, conv_weight, norm_gain):
    rows = log_decay.shape[0]
    blocks = rows // Q
    steps = log_decay.T.reshape(2, blocks, Q).transpose(1, 0, 2)
    steps = jnp.pad(steps, ((0, 0), (0, 6), (0, 0)))
    width = 2 * P_SIZE
    mine = lax.dynamic_slice_in_dim(
        conv_weight, lax.axis_index("fsdp") * width, width, axis=1
    )
    return steps, jnp.pad(mine, ((0, 4), (0, 0))), jnp.broadcast_to(norm_gain, (8, width))


def body(tokens, w_in, conv_weight, log_decay, norm_gain):
    tok_rows = tokens.shape[0]
    projected = jnp.dot(
        tokens,
        lax.all_gather(w_in, "fsdp", axis=0, tiled=True),
        preferred_element_type=F32,
    ).astype(BF16)
    heads = lax.all_to_all(
        projected[:, : H * P_SIZE], "fsdp", split_axis=1, concat_axis=0, tiled=True
    )
    state_part = projected[:, H * P_SIZE :]
    state_taps = conv_weight[:, H * P_SIZE :]
    rim = shifted(state_part[tok_rows - 3 :], ("ctx", "fsdp"), 1)
    extended = jnp.concatenate([rim, state_part], axis=0).astype(F32)
    summed = jnp.zeros((tok_rows, 2 * N), F32)
    for k in range(4):
        summed = summed + state_taps[k] * extended[k : k + tok_rows]
    state_rows = lax.all_gather(
        jax.nn.silu(summed).astype(BF16), "fsdp", axis=0, tiled=True
    )
    steps, taps, gain = scan_operands(log_decay, conv_weight, norm_gain)
    return scan(lax.axis_size("ctx"), heads, state_rows, steps, taps, gain)


def solution(mesh):
    placed = (P(("ctx", "fsdp"), None), P("fsdp", None), P(), P("ctx", "fsdp"), P("fsdp"))
    return jax.shard_map(
        body, mesh=mesh, in_specs=placed, out_specs=P("ctx", "fsdp"), check_vma=False
    )
```

time: 452 us -> 339 us (0.75)
  local copies, waits for them, and re-layouts: 96.5 us -> 6.46 us
  Pallas kernels: 0 us -> 44.7 us
  matrix products: 42.2 us -> 10.7 us
  blocking collectives: 30.9 us -> 0 us
  other arithmetic: 27.3 us -> 0.86 us
  waiting for transfers between devices: 232 us -> 256 us
    pad x8 -> x2, local copies, waits for them, and re-layouts: 48 us -> 0.73 us  [the longest x1 0.72 us: scan_operands(): steps = jnp.pad(steps, ((0, 0), (0, 6), (0, 0)))]
    pallas_call x0 -> x1, Pallas kernels: none -> 44.7 us  [scan(): pl.pallas_call(functools.partial(scan_kernel, n_ctx, blocks), out_shape=j...]
    dot_general x14 -> x0, matrix products: 31.6 us -> none  [the longest x4 10.6 us: group_outputs(): jnp.einsum('gtn,ghpn->gthp', c_part.astype(jnp.float32), start_part, prec...]
    all_to_all x1, waiting for transfers between devices: 30.5 us -> 52.4 us  [body(): lax.all_to_all(projected[:, :H * P_SIZE], 'fsdp', split_axis=1, concat_ax...]
    all_gather x1 -> x0, blocking collectives: 16.9 us -> none  [carried_in(): lax.all_gather(part.astype(kind), axis)]
    convert_element_type x2 -> x0, local copies, waits for them, and re-layouts: 15.6 us -> none  [body(): return normed.reshape(ctx_rows, heads_dev * P_SIZE).astype(jnp.bfloat16)]
    unnamed x1 -> x0, blocking collectives: 14 us -> none
    add x12 -> x0, other arithmetic: 13.1 us -> none  [the longest x5 8.18 us: body(): lax.associative_scan(combine_carry, (jnp.exp(totals), contribution), axis=0)]
  transfers between devices with their start and end apart: 4 -> 4, of which waited for: 4 -> 4; matrix products, arithmetic and copies ran while one was open for 3% -> 1% of each run, Pallas kernels for 0% -> 0%
where the time goes in v1:
time: 339 us; the launch traced here: 338 us
  waiting for transfers between devices  256 us (76%)
  Pallas kernels  44.7 us (13%)
  between operations  13.5 us (4%)
  matrix products  10.7 us (3%)
  local copies, waits for them, and re-layouts  6.46 us (2%)
  starting transfers between devices  6.11 us (2%)
    all_gather x1, waiting for transfers between devices, body(): lax.all_gather(w_in, 'fsdp', axis=0, tiled=True)  174 us
    all_to_all x1, waiting for transfers between devices, body(): lax.all_to_all(projected[:, :H * P_SIZE], 'fsdp', split_axis=1, concat_ax...  52.4 us
    pallas_call x1, Pallas kernels, scan(): pl.pallas_call(functools.partial(scan_kernel, n_ctx, blocks), out_shape=j...  44.7 us
    all_gather x1, waiting for transfers between devices, body(): lax.all_gather(jax.nn.silu(summed).astype(BF16), 'fsdp', axis=0, tiled=True)  22.9 us
    dot_general x1, matrix products, body(): jnp.dot(tokens, lax.all_gather(w_in, 'fsdp', axis=0, tiled=True), preferr...  10.7 us
  transfers between devices with their start and end apart: 4, of which 4 were waited for; matrix products, arithmetic and copies ran while one was open for 1% of the time, Pallas kernels for 0%

profile of v1, /device:TPU:1, one launch (start us, length us, event | category | flops | bytes accessed | tf_op | source)
XLA Modules:
  0.0 338.2 jit_solution(8689257651584057323)
XLA Ops:
  6.5 0.0 copy-start
  6.5 0.0 all-gather.3.cloned.1.call-start
  6.5 0.7 all-gather.3.cloned.1.call-update
  7.3 0.0 all-gather.5.cloned.1.call-start
  7.3 174.5 %all-gather.3.cloned.1.call-done = bf16[2560,4352]{1,0:T(8,128)(2,1)} async-done(((bf16[80,4352]{1,0:T(8,128)(2,1)}), bf16[2560,4352]{1,0:T(8,128)(2,1)}) %all-gather.3.cloned.1.call-update) | async-done | bytes 22282256 | tf_op jit(solution)/shard_map/all_gather | solution.py:252
  181.8 0.0 copy-done
  181.8 10.7 %convolution_convert_fusion = bf16[256,4352]{1,0:T(8,128)(2,1)S(1)} fusion(bf16[256,2560]{1,0:T(8,128)(2,1)S(1)} %copy-done, bf16[2560,4352]{1,0:T(8,128)(2,1)} %all-gather.3.cloned.1.call-done), kind=kOutput, calls=%fused_computation | convolution fusion | flops 5705367552 | bytes 25821184 | tf_op jit(solution)/shard_map/dot_general | solution.py:250
  192.4 1.9 collective-permute-start
  194.4 0.8 fusion.3
  195.2 5.4 %collective-permute-done = bf16[3,256]{1,0:T(4,128)(2,1)S(1)} collective-permute-done((bf16[3,256]{1,0:T(4,128)(2,1)S(1)}, bf16[3,256]{1,0:T(4,128)(2,1)S(1)}, u32[]{:S(2)}, u32[]{:S(2)}) %collective-permute-start) | collective-permute-done | bytes 1568 | tf_op jit(solution)/shard_map/ppermute | solution.py:233
  200.7 0.8 multiply_convert_fusion
  201.5 0.0 all-gather.5.cloned.1.call-update
  201.5 1.9 copy_bitcast_fusion
  203.4 0.0 copy-start.2
  203.4 0.0 copy-start.3
  203.5 4.1 %all-to-all-start = ((bf16[256,32,128]{2,0,1:T(8,128)(2,1)}), bf16[256,32,128]{2,0,1:T(8,128)(2,1)S(1)}, u32[]{:S(2)}, u32[]{:S(2)}) async-start(bf16[256,32,128]{2,0,1:T(8,128)(2,1)} %copy_bitcast_fusion), calls=%async_computation | async-start | bytes 4194304 | tf_op jit(solution)/shard_map/all_to_all | solution.py:255
  207.6 0.7 constant_dynamic-slice_fusion
  208.3 0.0 copy-done.2
  208.3 0.7 pad.8.decay
  209.0 52.4 %all-to-all-done = bf16[256,32,128]{2,0,1:T(8,128)(2,1)S(1)} async-done(((bf16[256,32,128]{2,0,1:T(8,128)(2,1)}), bf16[256,32,128]{2,0,1:T(8,128)(2,1)S(1)}, u32[]{:S(2)}, u32[]{:S(2)}) %all-to-all-start) | async-done | bytes 2097184 | tf_op jit(solution)/shard_map/all_to_all | solution.py:255
  261.5 22.9 %all-gather.5.cloned.1.call-done.bc = bf16[8192,256]{1,0:T(8,128)(2,1)} async-done(((bf16[256,256]{1,0:T(8,128)(2,1)}), bf16[8192,256]{1,0:T(8,128)(2,1)}) %all-gather.5.cloned.1.call-update) | async-done | bytes 4194320 | tf_op jit(solution)/shard_map/all_gather | solution.py:265
  284.4 0.0 copy-done.3
  284.4 0.0 copy-start.1
  284.4 0.9 copy-done.1
  285.3 44.7 %shard_map.55 = bf16[8192,128]{1,0:T(8,128)(2,1)S(1)} custom-call(bf16[8192,128]{1,0:T(8,128)(2,1)S(1)} %bitcast.19, bf16[8192,256]{1,0:T(8,128)(2,1)} %all-gather.5.cloned.1.call-done.bc, f32[32,8,256]{2,1,0:T(8,128)S(1)} %copy-done.1, f32[8,128]{1,0:T(8,128)S(1)} %pad.9.taps, f32[8,128]{1,0:T(8,128)S(1)} %broadcast_in_dim.3.gain), custom_call_target="tpu_custom_call" | custom-call | tf_op jit(solution)/shard_map/pallas_call | solution.py:206
  330.0 1.3 copy.11
  (5 shorter events, 0.1 us)
Async XLA Ops:
  6.5 175.2 %copy-start = (bf16[256,2560]{1,0:T(8,128)(2,1)S(1)}, bf16[256,2560]{1,0:T(8,128)(2,1)}, u32[]{:S(2)}) copy-start(bf16[256,2560]{1,0:T(8,128)(2,1)} %param.5) | copy-start | bytes 3932164
  6.5 175.2 %all-gather.3.cloned.1.call-start = ((), (), s32[]{:S(2)}) async-start(), calls=%async_computation.1 | async-start | bytes 22978560 | tf_op jit(solution)/shard_map/all_gather | solution.py:252
  7.3 277.1 %all-gather.5.cloned.1.call-start = ((), (), s32[]{:S(2)}) async-start(), calls=%async_computation.2 | async-start | bytes 4325376 | tf_op jit(solution)/shard_map/all_gather | solution.py:265
  192.4 8.2 %collective-permute-start = (bf16[3,256]{1,0:T(4,128)(2,1)S(1)}, bf16[3,256]{1,0:T(4,128)(2,1)S(1)}, u32[]{:S(2)}, u32[]{:S(2)}) collective-permute-start(bf16[3,256]{1,0:T(4,128)(2,1)S(1)} %slice.51), channel_id=1, source_target_pairs={{0,1},{1,2},{2,3},{3,4},{4,5},{5,6},{6,7},{7,8},{8,9},{9,10},{10,1... | collective-permute-start | bytes 4616 | tf_op jit(solution)/shard_map/ppermute | solution.py:233
  203.4 4.9 %copy-start.2 = (f32[8192,2]{0,1:T(2,128)S(1)}, f32[8192,2]{0,1:T(2,128)}, u32[]{:S(2)}) copy-start(f32[8192,2]{0,1:T(2,128)} %param.8) | copy-start | bytes 196612
  203.4 80.9 %copy-start.3 = (f32[128]{0:T(128)S(1)}, f32[128]{0:T(128)}, u32[]{:S(2)}) copy-start(f32[128]{0:T(128)} %param.9) | copy-start | bytes 1540
  203.5 58.0 %all-to-all-start = ((bf16[256,32,128]{2,0,1:T(8,128)(2,1)}), bf16[256,32,128]{2,0,1:T(8,128)(2,1)S(1)}, u32[]{:S(2)}, u32[]{:S(2)}) async-start(bf16[256,32,128]{2,0,1:T(8,128)(2,1)} %copy_bitcast_fusion), calls=%async_computation | async-start | bytes 4194304 | tf_op jit(solution)/shard_map/all_to_all | solution.py:255
  284.4 1.0 copy-start.1
Sparse Core Ops, SparseCore 0:
  9.9 171.7 all-gather.2
  201.7 82.6 all-gather.4

commit v2 on v1

--- a/solution.py
+++ b/solution.py
@@ -227,10 +227,470 @@
     )(proj, bc, decay, taps, gain)
 
 
-def shifted(block, axis, distance):
-    devices = range(lax.axis_size(axis))
-    route = [(i - distance, i) for i in devices if i - distance in devices]
-    return lax.ppermute(block, axis, route)
+NX, NY, NZ = 4, 4, 8
+ROWS = 256
+DEPTH = 2560
+SHARD = 80
+HEAD_COLUMNS = 1024
+STATE_AT = 4096
+
+
+def exchange_kernel(
+    tokens,
+    w_in,
+    taps,
+    proj,
+    bc,
+    tok,
+    weights,
+    state_weights,
+    pieces,
+    halo,
+    own_sems,
+    halo_sems,
+    tok_send,
+    tok_recv,
+    shard_sems,
+    x_send,
+    x_recv,
+    core_send,
+    core_recv,
+    ring_send,
+    ring_recv,
+    bc_send,
+    bc_recv,
+    out_send,
+    out_recv,
+):
+    ctx = lax.axis_index("ctx")
+    f = lax.axis_index("fsdp")
+    x, c = ctx // 2, lax.rem(ctx, 2)
+    y, z = f // NZ, lax.rem(f, NZ)
+
+    def at(dx=0, dc=0, dy=0, dz=0):
+        return {
+            "ctx": lax.rem(x + dx, NX) * 2 + lax.rem(c + dc, 2),
+            "fsdp": lax.rem(y + dy, NY) * NZ + lax.rem(z + dz, NZ),
+        }
+
+    def remote(source, target, send_sem, recv_sem, device):
+        return pltpu.make_async_remote_copy(
+            src_ref=source,
+            dst_ref=target,
+            send_sem=send_sem,
+            recv_sem=recv_sem,
+            device_id=device,
+            device_id_type=MESH,
+        )
+
+    def settle(ref, sem):
+        pltpu.make_async_copy(ref, ref, sem).wait()
+
+    def columns(index):
+        return pl.ds(pl.multiple_of(index * 128, 128), 128)
+
+    def shard(index):
+        return pl.ds(pl.multiple_of(index * SHARD, 16), SHARD)
+
+    def block(index):
+        return pl.ds(pl.multiple_of(index * Q, Q), Q)
+
+    half = columns(c)
+    other_half = columns(1 - c)
+    devices = NY * NZ
+
+    barrier = pltpu.get_barrier_semaphore()
+
+    def greet(device):
+        pl.semaphore_signal(barrier, inc=1, device_id=device, device_id_type=MESH)
+
+    def greet_row(r, _):
+        greet({"ctx": ctx, "fsdp": lax.rem(f + r, devices)})
+        return 0
+
+    lax.fori_loop(1, devices, greet_row, 0)
+    for dx in range(1, NX):
+        greet(at(dx=dx))
+    greet(at(dc=1))
+    greet(
+        {
+            "ctx": lax.rem(ctx + 2 * NX - (devices - f) // devices, 2 * NX),
+            "fsdp": lax.rem(f + devices - 1, devices),
+        }
+    )
+    own_tokens = pltpu.make_async_copy(tokens, tok.at[0], own_sems.at[0])
+    own_tokens.start()
+    own_column = NZ * y + lax.rem(2 * x + c + z, NZ)
+    own_shard = pltpu.make_async_copy(
+        w_in.at[:, columns(own_column)],
+        weights.at[0, shard(f), half],
+        own_sems.at[1],
+    )
+    own_shard.start()
+    own_state_shard = pltpu.make_async_copy(
+        w_in.at[:, columns(STATE_AT // 128 + c)],
+        state_weights.at[shard(f), half],
+        own_sems.at[2],
+    )
+    gives_state = lax.rem(z, NX) == x
+
+    @pl.when(gives_state)
+    def _():
+        own_state_shard.start()
+
+    pl.semaphore_wait(barrier, devices - 1 + NX - 1 + 2)
+
+    def give_shard(r, _):
+        other = lax.rem(f + r, devices)
+        column = NZ * (other // NZ) + lax.rem(2 * x + c + lax.rem(other, NZ), NZ)
+        remote(
+            w_in.at[:, columns(column)],
+            weights.at[0, shard(f), half],
+            shard_sems.at[0],
+            shard_sems.at[1],
+            {"ctx": ctx, "fsdp": other},
+        ).start()
+        return 0
+
+    def state_shard_copy(r):
+        return remote(
+            w_in.at[:, columns(STATE_AT // 128 + c)],
+            state_weights.at[shard(f), half],
+            shard_sems.at[2],
+            shard_sems.at[3],
+            {"ctx": ctx, "fsdp": lax.rem(f + r, devices)},
+        )
+
+    def give_state_shard(r, _):
+        state_shard_copy(r).start()
+        return 0
+
+    lax.fori_loop(1, devices, give_shard, 0)
+
+    def tok_copy(slot, part, dy, target):
+        rows = pl.ds(part * (ROWS // 2), ROWS // 2)
+        source = tokens.at[rows] if slot == 0 else tok.at[slot, rows]
+        way = 0 if dy == 1 else 1
+        return remote(
+            source,
+            tok.at[target, rows],
+            tok_send.at[slot, way, part],
+            tok_recv.at[target, part],
+            at(dy=dy),
+        )
+
+    halo_copy = remote(
+        tokens.at[pl.ds(ROWS - HALO, HALO)],
+        halo,
+        halo_sems.at[0],
+        halo_sems.at[1],
+        {
+            "ctx": lax.rem(ctx + (f + 1) // devices, 2 * NX),
+            "fsdp": lax.rem(f + 1, devices),
+        },
+    )
+    halo_copy.start()
+    tok_copy(0, 0, 1, 3).start()
+    tok_copy(0, 1, 3, 1).start()
+    tok_copy(0, 1, 1, 3).start()
+    tok_copy(0, 0, 3, 1).start()
+
+    @pl.when(gives_state)
+    def _():
+        lax.fori_loop(1, devices, give_state_shard, 0)
+
+    def tok_arrived(slot, part):
+        settle(tok.at[slot, pl.ds(part * (ROWS // 2), ROWS // 2)], tok_recv.at[slot, part])
+
+    def x_copy(slot, dx, target, part):
+        rows = pl.ds(0, DEPTH) if part is None else pl.ds(part * (DEPTH // 2), DEPTH // 2)
+        way = 0 if dx == 1 else 1
+        return remote(
+            weights.at[slot, rows, half],
+            weights.at[target, rows, half],
+            x_send.at[slot, way],
+            x_recv.at[target, 0 if part is None else part],
+            at(dx=dx),
+        )
+
+    def core_copy(slot):
+        return remote(
+            weights.at[slot, :, half],
+            weights.at[slot, :, half],
+            core_send.at[slot],
+            core_recv.at[slot],
+            at(dc=1),
+        )
+
+    own_shard.wait()
+    settle(
+        weights.at[0, pl.ds(0, (devices - 1) * SHARD), half], shard_sems.at[1]
+    )
+    core_copy(0).start()
+    x_copy(0, 1, 3, None).start()
+    x_copy(0, 3, 1, None).start()
+
+    @pl.when(gives_state)
+    def _():
+        own_state_shard.wait()
+        settle(state_weights.at[pl.ds(0, 7 * SHARD), half], shard_sems.at[3])
+
+    @pl.when(jnp.logical_not(gives_state))
+    def _():
+        settle(state_weights.at[pl.ds(0, 8 * SHARD), half], shard_sems.at[3])
+
+    def give_plane(i, _):
+        rows = shard(lax.rem(i, 8) // 2 * NZ + x + NX * lax.rem(i, 2))
+        remote(
+            state_weights.at[rows, half],
+            state_weights.at[rows, half],
+            shard_sems.at[4],
+            shard_sems.at[5],
+            at(dx=1 + i // 8),
+        ).start()
+        return 0
+
+    lax.fori_loop(0, 24, give_plane, 0)
+
+    tok_arrived(3, 0)
+    tok_copy(3, 0, 1, 2).start()
+    tok_arrived(1, 1)
+    tok_copy(1, 1, 3, 2).start()
+
+    settle(state_weights.at[pl.ds(0, 24 * SHARD), half], shard_sems.at[5])
+    state_core = remote(
+        state_weights.at[:, half],
+        state_weights.at[:, half],
+        core_send.at[4],
+        core_recv.at[4],
+        at(dc=1),
+    )
+    state_core.start()
+    halo_copy.wait_recv()
+    settle(state_weights.at[:, other_half], core_recv.at[4])
+
+    own_tokens.wait()
+    before = jnp.dot(halo[...], state_weights[...], preferred_element_type=F32)
+    before = jnp.where(ctx + f == 0, 0.0, before.astype(BF16).astype(F32))
+    here = jnp.dot(tok[0], state_weights[...], preferred_element_type=F32)
+    window = jnp.concatenate(
+        [before[HALO - 8 :], here.astype(BF16).astype(F32)], axis=0
+    )
+    summed = taps[0:1] * window[5 : 5 + ROWS]
+    for k in range(1, 4):
+        summed = summed + taps[k : k + 1] * window[5 + k : 5 + k + ROWS]
+    bc[block(f), :] = jax.nn.silu(summed).astype(BF16)
+
+    def bc_rows(t, k):
+        return lax.rem(y + t, NY) * NZ + lax.rem(z + k, NZ)
+
+    def ring_copy(k, way):
+        rows = bc.at[block(bc_rows(0, k))]
+        target = (k + 7) % 8 if way == 0 else k + 1
+        return remote(
+            rows,
+            rows,
+            ring_send.at[k, way],
+            ring_recv.at[target],
+            at(dz=1 if way == 0 else NZ - 1),
+        )
+
+    def bc_copy(t, k, way):
+        index = bc_rows(t, k)
+        if t == 0:
+            rows, part = bc.at[block(index)], 0
+        else:
+            part = way
+            rows = bc.at[
+                pl.ds(pl.multiple_of(index * Q + part * (Q // 2), Q // 2), Q // 2)
+            ]
+        target = (3 if way == 0 else 1) if t == 0 else 2
+        return remote(
+            rows,
+            rows,
+            bc_send.at[t, k, way],
+            bc_recv.at[target, k, part],
+            at(dy=1 if way == 0 else NY - 1),
+        )
+
+    def ring_arrived(k):
+        settle(bc.at[block(bc_rows(0, k))], ring_recv.at[k])
+
+    def bc_on(k):
+        bc_copy(0, k, 0).start()
+        bc_copy(0, k, 1).start()
+
+    ring_copy(0, 0).start()
+    ring_copy(0, 1).start()
+    bc_on(0)
+
+    def out_piece(t, s, side):
+        away = lax.rem(2 * lax.rem(x + s, NX) + side, NZ)
+        rows = block(lax.rem(y + t, NY) * NZ + z)
+        return pieces.at[t, s, :, pl.ds(side * 128, 128)], rows, away
+
+    def multiply(t, s):
+        product = jnp.dot(tok[t], weights[s], preferred_element_type=F32)
+        pieces[t, s] = product.astype(BF16)
+        for side in range(2):
+            source, rows, away = out_piece(t, s, side)
+
+            @pl.when(away == 0)
+            def _():
+                pltpu.make_async_copy(source, proj.at[rows], out_send.at[0, t]).start()
+
+            @pl.when(away != 0)
+            def _():
+                remote(
+                    source,
+                    proj.at[rows],
+                    out_send.at[away, t],
+                    out_recv.at[away, t],
+                    {"ctx": ctx, "fsdp": y * NZ + lax.rem(z + away, NZ)},
+                ).start()
+
+    def core_arrived(slot):
+        settle(weights.at[slot, :, other_half], core_recv.at[slot])
+
+    core_arrived(0)
+    multiply(0, 0)
+    ring_arrived(7)
+    ring_copy(7, 0).start()
+    ring_arrived(1)
+    ring_copy(1, 1).start()
+    bc_on(7)
+    bc_on(1)
+    tok_arrived(3, 1)
+    multiply(3, 0)
+    tok_arrived(1, 0)
+    multiply(1, 0)
+    ring_arrived(6)
+    ring_copy(6, 0).start()
+    ring_arrived(2)
+    ring_copy(2, 1).start()
+    bc_on(6)
+    bc_on(2)
+    settle(weights.at[3, :, half], x_recv.at[3, 0])
+    x_copy(3, 1, 2, 0).start()
+    core_copy(3).start()
+    settle(weights.at[1, :, half], x_recv.at[1, 0])
+    x_copy(1, 3, 2, 1).start()
+    core_copy(1).start()
+    core_arrived(3)
+    multiply(0, 3)
+    ring_arrived(5)
+    ring_copy(5, 0).start()
+    ring_arrived(3)
+    bc_on(5)
+    bc_on(3)
+    core_arrived(1)
+    multiply(0, 1)
+    multiply(3, 3)
+    multiply(3, 1)
+    multiply(1, 3)
+    multiply(1, 1)
+    ring_arrived(4)
+    bc_on(4)
+    settle(weights.at[2, pl.ds(0, DEPTH // 2), half], x_recv.at[2, 0])
+    settle(weights.at[2, pl.ds(DEPTH // 2, DEPTH // 2), half], x_recv.at[2, 1])
+    core_copy(2).start()
+    core_arrived(2)
+    multiply(0, 2)
+    multiply(3, 2)
+    multiply(1, 2)
+    tok_arrived(2, 0)
+    tok_arrived(2, 1)
+    multiply(2, 0)
+    multiply(2, 3)
+    multiply(2, 1)
+    multiply(2, 2)
+
+    for k in (0, 7, 1, 6, 2, 5, 3, 4):
+        settle(bc.at[block(bc_rows(3, k))], bc_recv.at[3, k, 0])
+        bc_copy(3, k, 0).start()
+        settle(bc.at[block(bc_rows(1, k))], bc_recv.at[1, k, 0])
+        bc_copy(1, k, 1).start()
+
+    for k in range(8):
+        for way in range(2):
+            bc_copy(0, k, way).wait_send()
+            bc_copy(3 if way == 0 else 1, k, way).wait_send()
+            index = bc_rows(2, k)
+            settle(
+                bc.at[pl.ds(pl.multiple_of(index * Q + way * (Q // 2), Q // 2), Q // 2)],
+                bc_recv.at[2, k, way],
+            )
+    for k, way in ((0, 0), (0, 1), (7, 0), (1, 1), (6, 0), (2, 1), (5, 0)):
+        ring_copy(k, way).wait_send()
+    for slot in range(4):
+        core_copy(slot).wait_send()
+    state_core.wait_send()
+    x_copy(0, 1, 3, None).wait_send()
+    x_copy(0, 3, 1, None).wait_send()
+    x_copy(3, 1, 2, 0).wait_send()
+    x_copy(1, 3, 2, 1).wait_send()
+    for part in range(2):
+        tok_copy(0, part, 1, 3).wait_send()
+        tok_copy(0, part, 3, 1).wait_send()
+    tok_copy(3, 0, 1, 2).wait_send()
+    tok_copy(1, 1, 3, 2).wait_send()
+    halo_copy.wait_send()
+    settle(weights.at[0, pl.ds(0, (devices - 1) * SHARD), half], shard_sems.at[0])
+    settle(state_weights.at[pl.ds(0, 24 * SHARD), half], shard_sems.at[4])
+
+    @pl.when(gives_state)
+    def _():
+        settle(
+            state_weights.at[pl.ds(0, (devices - 1) * SHARD), half], shard_sems.at[2]
+        )
+
+    for t in range(NY):
+        rows = lax.rem(y + t, NY) * NZ
+        settle(proj.at[block(rows + z)], out_send.at[0, t])
+        for away in range(1, NZ):
+            settle(proj.at[block(rows + z)], out_send.at[away, t])
+            source = lax.rem(z + NZ - away, NZ)
+            settle(proj.at[block(rows + source)], out_recv.at[away, t])
+
+
+def exchange(tokens, w_in, taps):
+    vmem = pl.BlockSpec(memory_space=pltpu.VMEM)
+    dma = pltpu.SemaphoreType.DMA
+    blocks = NY * NZ
+    return pl.pallas_call(
+        exchange_kernel,
+        out_shape=[
+            jax.ShapeDtypeStruct((blocks * Q, 2 * P_SIZE), BF16),
+            jax.ShapeDtypeStruct((blocks * Q, 2 * N), BF16),
+        ],
+        in_specs=[vmem] * 3,
+        out_specs=[vmem] * 2,
+        scratch_shapes=[
+            pltpu.VMEM((NY, ROWS, DEPTH), BF16),
+            pltpu.VMEM((NX, DEPTH, 256), BF16),
+            pltpu.VMEM((DEPTH, 2 * N), BF16),
+            pltpu.VMEM((NY, NX, ROWS, 256), BF16),
+            pltpu.VMEM((HALO, DEPTH), BF16),
+            dma((3,)),
+            dma((2,)),
+            dma((4, 2, 2)),
+            dma((4, 2)),
+            dma((6,)),
+            dma((4, 2)),
+            dma((4, 2)),
+            dma((5,)),
+            dma((5,)),
+            dma((8, 2)),
+            dma((8,)),
+            dma((4, 8, 2)),
+            dma((4, 8, 2)),
+            dma((8, 4)),
+            dma((8, 4)),
+        ],
+        compiler_params=pltpu.CompilerParams(
+            collective_id=2, has_side_effects=True, vmem_limit_bytes=48 * 2**20
+        ),
+    )(tokens, w_in, taps)
 
 
 def scan_operands(log_decay, conv_weight, norm_gain):
@@ -246,25 +706,8 @@
 
 
 def body(tokens, w_in, conv_weight, log_decay, norm_gain):
-    tok_rows = tokens.shape[0]
-    projected = jnp.dot(
-        tokens,
-        lax.all_gather(w_in, "fsdp", axis=0, tiled=True),
-        preferred_element_type=F32,
-    ).astype(BF16)
-    heads = lax.all_to_all(
-        projected[:, : H * P_SIZE], "fsdp", split_axis=1, concat_axis=0, tiled=True
-    )
-    state_part = projected[:, H * P_SIZE :]
-    state_taps = conv_weight[:, H * P_SIZE :]
-    rim = shifted(state_part[tok_rows - 3 :], ("ctx", "fsdp"), 1)
-    extended = jnp.concatenate([rim, state_part], axis=0).astype(F32)
-    summed = jnp.zeros((tok_rows, 2 * N), F32)
-    for k in range(4):
-        summed = summed + state_taps[k] * extended[k : k + tok_rows]
-    state_rows = lax.all_gather(
-        jax.nn.silu(summed).astype(BF16), "fsdp", axis=0, tiled=True
-    )
+    state_taps = jnp.pad(conv_weight[:, STATE_AT:], ((0, 4), (0, 0)))
+    heads, state_rows = exchange(tokens, w_in, state_taps)
     steps, taps, gain = scan_operands(log_decay, conv_weight, norm_gain)
     return scan(lax.axis_size("ctx"), heads, state_rows, steps, taps, gain)
 

time: 339 us -> 184 us (0.54)
  waiting for transfers between devices: 256 us -> 0 us
  Pallas kernels: 44.7 us -> 176 us
  between operations: 13.5 us -> 0.03 us
  matrix products: 10.7 us -> 0 us
  starting transfers between devices: 6.11 us -> 0 us
    all_gather x2 -> x0, waiting for transfers between devices: 197 us -> none  [the longest x1 174 us: body(): lax.all_gather(w_in, 'fsdp', axis=0, tiled=True)]
    pallas_call x0 -> x1, Pallas kernels: none -> 126 us  [exchange(): pl.pallas_call(exchange_kernel, out_shape=[jax.ShapeDtypeStruct((blocks *...]
    all_to_all x1 -> x0, waiting for transfers between devices: 52.4 us -> none  [body(): lax.all_to_all(projected[:, :H * P_SIZE], 'fsdp', split_axis=1, concat_ax...]
    dot_general x1 -> x0, matrix products: 10.7 us -> none  [body(): jnp.dot(tokens, lax.all_gather(w_in, 'fsdp', axis=0, tiled=True), preferr...]
    pallas_call x1, Pallas kernels: 44.7 us -> 50.6 us  [scan(): pl.pallas_call(functools.partial(scan_kernel, n_ctx, blocks), out_shape=j...]
    ppermute x1 -> x0, waiting for transfers between devices: 5.44 us -> none  [shifted(): return lax.ppermute(block, axis, route)]
    all_to_all x1 -> x0, starting transfers between devices: 4.14 us -> none  [body(): lax.all_to_all(projected[:, :H * P_SIZE], 'fsdp', split_axis=1, concat_ax...]
  transfers between devices with their start and end apart: 4 -> 0, of which waited for: 4 -> 0; matrix products, arithmetic and copies ran while one was open for 1% -> 0% of each run, Pallas kernels for 0% -> 0%
where the time goes in v2:
time: 184 us; the launch traced here: 183 us
  Pallas kernels  176 us (96%)
  local copies, waits for them, and re-layouts  6.63 us (4%)
    pallas_call x1, Pallas kernels, exchange(): pl.pallas_call(exchange_kernel, out_shape=[jax.ShapeDtypeStruct((blocks *...  126 us
    pallas_call x1, Pallas kernels, scan(): pl.pallas_call(functools.partial(scan_kernel, n_ctx, blocks), out_shape=j...  50.6 us
    unnamed x5, local copies, waits for them, and re-layouts  3.73 us

profile of v2, /device:TPU:1, one launch (start us, length us, event | category | flops | bytes accessed | tf_op | source)
XLA Modules:
  0.0 183.1 jit_solution(5771877728382013038)
XLA Ops:
  0.0 0.7 constant_dynamic-slice_fusion
  0.7 0.7 broadcast_in_dim.3.gain
  1.3 0.7 slice.3
  2.0 0.9 pad.13.decay
  2.9 0.0 copy-start
  2.9 1.3 copy-done
  4.2 0.0 copy-start.1
  4.2 1.1 copy-done.1
  5.3 125.9 %shard_map.55 = (bf16[8192,128]{1,0:T(8,128)(2,1)S(1)}, bf16[8192,256]{1,0:T(8,128)(2,1)}) custom-call(bf16[256,2560]{1,0:T(8,128)(2,1)S(1)} %copy-done, bf16[80,4352]{1,0:T(8,128)(2,1)S(1)} %copy-done.1, f32[8,256]{1,0:T(8,128)S(1)} %pad.12.taps), custom_call_target="tpu_custom_call" | custom-call | tf_op jit(solution)/shard_map/pallas_call | solution.py:660
  131.2 50.6 %shard_map.56 = bf16[8192,128]{1,0:T(8,128)(2,1)S(1)} custom-call(bf16[8192,128]{1,0:T(8,128)(2,1)S(1)} %get-tuple-element.7.proj, bf16[8192,256]{1,0:T(8,128)(2,1)} %get-tuple-element.8.bc, f32[32,8,256]{2,1,0:T(8,128)S(1)} %pad.13.decay, f32[8,128]{1,0:T(8,128)S(1)} %pad.14.taps, f32[8,128]{1,0:T(8,128)S(1)} %broadcast_in_dim.3.gain), custom_call_target="tpu_custom_call" | custom-call | tf_op jit(solution)/shard_map/pallas_call | solution.py:206
  181.7 1.3 copy.7
  (2 shorter events, 0.0 us)
Async XLA Ops:
  2.9 1.3 copy-start
  4.2 1.1 copy-start.1

commit v3 on v2

--- a/solution.py
+++ b/solution.py
@@ -123,6 +123,7 @@
         blocks,
         states,
         (first, jnp.zeros((N, 2 * P_SIZE), F32), jnp.zeros((1, 2 * P_SIZE), F32)),
+        unroll=4,
     )
     mine[0:N] = state
     mine[N : N + 8] = jnp.broadcast_to(jnp.exp(offset), (8, 2 * P_SIZE))
@@ -163,7 +164,7 @@
         within[pl.ds(base, Q), :] = jnp.where(first_head, parts[0], parts[1])
         return 0
 
-    lax.fori_loop(0, blocks, inside, 0)
+    lax.fori_loop(0, blocks, inside, 0, unroll=4)
 
     for r in range(1, n_ctx):
         carry_copy(r).wait()
@@ -195,7 +196,7 @@
         out[pl.ds(base, Q), :] = normed.astype(BF16)
         return 0
 
-    lax.fori_loop(0, blocks, finish, 0)
+    lax.fori_loop(0, blocks, finish, 0, unroll=4)
 
 
 def scan(n_ctx, proj, bc, decay, taps, gain):
@@ -365,6 +366,10 @@
         state_shard_copy(r).start()
         return 0
 
+    @pl.when(gives_state)
+    def _():
+        lax.fori_loop(1, devices, give_state_shard, 0)
+
     lax.fori_loop(1, devices, give_shard, 0)
 
     def tok_copy(slot, part, dy, target):
@@ -395,10 +400,6 @@
     tok_copy(0, 1, 1, 3).start()
     tok_copy(0, 0, 3, 1).start()
 
-    @pl.when(gives_state)
-    def _():
-        lax.fori_loop(1, devices, give_state_shard, 0)
-
     def tok_arrived(slot, part):
         settle(tok.at[slot, pl.ds(part * (ROWS // 2), ROWS // 2)], tok_recv.at[slot, part])
 
@@ -421,65 +422,6 @@
             core_recv.at[slot],
             at(dc=1),
         )
-
-    own_shard.wait()
-    settle(
-        weights.at[0, pl.ds(0, (devices - 1) * SHARD), half], shard_sems.at[1]
-    )
-    core_copy(0).start()
-    x_copy(0, 1, 3, None).start()
-    x_copy(0, 3, 1, None).start()
-
-    @pl.when(gives_state)
-    def _():
-        own_state_shard.wait()
-        settle(state_weights.at[pl.ds(0, 7 * SHARD), half], shard_sems.at[3])
-
-    @pl.when(jnp.logical_not(gives_state))
-    def _():
-        settle(state_weights.at[pl.ds(0, 8 * SHARD), half], shard_sems.at[3])
-
-    def give_plane(i, _):
-        rows = shard(lax.rem(i, 8) // 2 * NZ + x + NX * lax.rem(i, 2))
-        remote(
-            state_weights.at[rows, half],
-            state_weights.at[rows, half],
-            shard_sems.at[4],
-            shard_sems.at[5],
-            at(dx=1 + i // 8),
-        ).start()
-        return 0
-
-    lax.fori_loop(0, 24, give_plane, 0)
-
-    tok_arrived(3, 0)
-    tok_copy(3, 0, 1, 2).start()
-    tok_arrived(1, 1)
-    tok_copy(1, 1, 3, 2).start()
-
-    settle(state_weights.at[pl.ds(0, 24 * SHARD), half], shard_sems.at[5])
-    state_core = remote(
-        state_weights.at[:, half],
-        state_weights.at[:, half],
-        core_send.at[4],
-        core_recv.at[4],
-        at(dc=1),
-    )
-    state_core.start()
-    halo_copy.wait_recv()
-    settle(state_weights.at[:, other_half], core_recv.at[4])
-
-    own_tokens.wait()
-    before = jnp.dot(halo[...], state_weights[...], preferred_element_type=F32)
-    before = jnp.where(ctx + f == 0, 0.0, before.astype(BF16).astype(F32))
-    here = jnp.dot(tok[0], state_weights[...], preferred_element_type=F32)
-    window = jnp.concatenate(
-        [before[HALO - 8 :], here.astype(BF16).astype(F32)], axis=0
-    )
-    summed = taps[0:1] * window[5 : 5 + ROWS]
-    for k in range(1, 4):
-        summed = summed + taps[k : k + 1] * window[5 + k : 5 + k + ROWS]
-    bc[block(f), :] = jax.nn.silu(summed).astype(BF16)
 
     def bc_rows(t, k):
         return lax.rem(y + t, NY) * NZ + lax.rem(z + k, NZ)
@@ -520,10 +462,6 @@
         bc_copy(0, k, 0).start()
         bc_copy(0, k, 1).start()
 
-    ring_copy(0, 0).start()
-    ring_copy(0, 1).start()
-    bc_on(0)
-
     def out_piece(t, s, side):
         away = lax.rem(2 * lax.rem(x + s, NX) + side, NZ)
         rows = block(lax.rem(y + t, NY) * NZ + z)
@@ -552,24 +490,93 @@
     def core_arrived(slot):
         settle(weights.at[slot, :, other_half], core_recv.at[slot])
 
-    core_arrived(0)
-    multiply(0, 0)
+    @pl.when(gives_state)
+    def _():
+        own_state_shard.wait()
+        settle(state_weights.at[pl.ds(0, 7 * SHARD), half], shard_sems.at[3])
+
+    @pl.when(jnp.logical_not(gives_state))
+    def _():
+        settle(state_weights.at[pl.ds(0, 8 * SHARD), half], shard_sems.at[3])
+
+    def give_plane(i, _):
+        rows = shard(lax.rem(i, 8) // 2 * NZ + x + NX * lax.rem(i, 2))
+        remote(
+            state_weights.at[rows, half],
+            state_weights.at[rows, half],
+            shard_sems.at[4],
+            shard_sems.at[5],
+            at(dx=1 + i // 8),
+        ).start()
+        return 0
+
+    lax.fori_loop(0, 24, give_plane, 0)
+
+    settle(state_weights.at[pl.ds(0, 24 * SHARD), half], shard_sems.at[5])
+    state_core = remote(
+        state_weights.at[:, half],
+        state_weights.at[:, half],
+        core_send.at[4],
+        core_recv.at[4],
+        at(dc=1),
+    )
+    state_core.start()
+    own_tokens.wait()
+    halo_copy.wait_recv()
+    settle(state_weights.at[:, other_half], core_recv.at[4])
+
+    before = jnp.dot(halo[...], state_weights[...], preferred_element_type=F32)
+    before = jnp.where(ctx + f == 0, 0.0, before.astype(BF16).astype(F32))
+    here = jnp.dot(tok[0], state_weights[...], preferred_element_type=F32)
+    window = jnp.concatenate(
+        [before[HALO - 8 :], here.astype(BF16).astype(F32)], axis=0
+    )
+    summed = taps[0:1] * window[5 : 5 + ROWS]
+    for k in range(1, 4):
+        summed = summed + taps[k : k + 1] * window[5 + k : 5 + k + ROWS]
+    bc[block(f), :] = jax.nn.silu(summed).astype(BF16)
+
+    ring_copy(0, 0).start()
+    ring_copy(0, 1).start()
+    own_shard.wait()
+    settle(
+        weights.at[0, pl.ds(0, (devices - 1) * SHARD), half], shard_sems.at[1]
+    )
+    core_copy(0).start()
+    x_copy(0, 1, 3, None).start()
+    x_copy(0, 3, 1, None).start()
+
+    tok_arrived(3, 0)
+    tok_copy(3, 0, 1, 2).start()
+    tok_arrived(1, 1)
+    tok_copy(1, 1, 3, 2).start()
+
     ring_arrived(7)
     ring_copy(7, 0).start()
     ring_arrived(1)
     ring_copy(1, 1).start()
+    core_arrived(0)
+    multiply(0, 0)
+    bc_on(0)
     bc_on(7)
     bc_on(1)
-    tok_arrived(3, 1)
-    multiply(3, 0)
-    tok_arrived(1, 0)
-    multiply(1, 0)
     ring_arrived(6)
     ring_copy(6, 0).start()
     ring_arrived(2)
     ring_copy(2, 1).start()
     bc_on(6)
     bc_on(2)
+    ring_arrived(5)
+    ring_copy(5, 0).start()
+    ring_arrived(3)
+    bc_on(5)
+    bc_on(3)
+    ring_arrived(4)
+    bc_on(4)
+    tok_arrived(3, 1)
+    multiply(3, 0)
+    tok_arrived(1, 0)
+    multiply(1, 0)
     settle(weights.at[3, :, half], x_recv.at[3, 0])
     x_copy(3, 1, 2, 0).start()
     core_copy(3).start()
@@ -578,19 +585,12 @@
     core_copy(1).start()
     core_arrived(3)
     multiply(0, 3)
-    ring_arrived(5)
-    ring_copy(5, 0).start()
-    ring_arrived(3)
-    bc_on(5)
-    bc_on(3)
+    multiply(3, 3)
+    multiply(1, 3)
     core_arrived(1)
     multiply(0, 1)
-    multiply(3, 3)
     multiply(3, 1)
-    multiply(1, 3)
     multiply(1, 1)
-    ring_arrived(4)
-    bc_on(4)
     settle(weights.at[2, pl.ds(0, DEPTH // 2), half], x_recv.at[2, 0])
     settle(weights.at[2, pl.ds(DEPTH // 2, DEPTH // 2), half], x_recv.at[2, 1])
     core_copy(2).start()

time: 184 us -> 149 us (0.81)
  Pallas kernels: 176 us -> 142 us
    pallas_call x1, Pallas kernels: 50.6 us -> 30.5 us  [scan(): pl.pallas_call(functools.partial(scan_kernel, n_ctx, blocks), out_shape=j...]
    pallas_call x1, Pallas kernels: 126 us -> 112 us  [exchange(): pl.pallas_call(exchange_kernel, out_shape=[jax.ShapeDtypeStruct((blocks *...]
where the time goes in v3:
time: 149 us
  Pallas kernels  142 us (95%)
  local copies, waits for them, and re-layouts  6.63 us (4%)
    pallas_call x1, Pallas kernels, exchange(): pl.pallas_call(exchange_kernel, out_shape=[jax.ShapeDtypeStruct((blocks *...  112 us
    pallas_call x1, Pallas kernels, scan(): pl.pallas_call(functools.partial(scan_kernel, n_ctx, blocks), out_shape=j...  30.5 us
    unnamed x5, local copies, waits for them, and re-layouts  3.73 us

profile of v3, /device:TPU:1, one launch (start us, length us, event | category | flops | bytes accessed | tf_op | source)
XLA Modules:
  0.0 149.1 jit_solution(12556460963742847565)
XLA Ops:
  0.0 0.7 constant_dynamic-slice_fusion
  0.7 0.7 broadcast_in_dim.3.gain
  1.3 0.7 slice.3
  2.0 0.9 pad.13.decay
  2.9 0.0 copy-start
  2.9 1.3 copy-done
  4.2 0.0 copy-start.1
  4.2 1.1 copy-done.1
  5.3 112.0 %shard_map.55 = (bf16[8192,128]{1,0:T(8,128)(2,1)S(1)}, bf16[8192,256]{1,0:T(8,128)(2,1)}) custom-call(bf16[256,2560]{1,0:T(8,128)(2,1)S(1)} %copy-done, bf16[80,4352]{1,0:T(8,128)(2,1)S(1)} %copy-done.1, f32[8,256]{1,0:T(8,128)S(1)} %pad.12.taps), custom_call_target="tpu_custom_call" | custom-call | tf_op jit(solution)/shard_map/pallas_call | solution.py:660
  117.3 30.5 %shard_map.56 = bf16[8192,128]{1,0:T(8,128)(2,1)S(1)} custom-call(bf16[8192,128]{1,0:T(8,128)(2,1)S(1)} %get-tuple-element.7.proj, bf16[8192,256]{1,0:T(8,128)(2,1)} %get-tuple-element.8.bc, f32[32,8,256]{2,1,0:T(8,128)S(1)} %pad.13.decay, f32[8,128]{1,0:T(8,128)S(1)} %pad.14.taps, f32[8,128]{1,0:T(8,128)S(1)} %broadcast_in_dim.3.gain), custom_call_target="tpu_custom_call" | custom-call | tf_op jit(solution)/shard_map/pallas_call | solution.py:207
  147.8 1.3 copy.7
  (2 shorter events, 0.0 us)
Async XLA Ops:
  2.9 1.3 copy-start
  4.2 1.1 copy-start.1

commit v4 on v3

--- a/solution.py
+++ b/solution.py
@@ -1,5 +1,3 @@
-import functools
-
 import jax
 import jax.numpy as jnp
 from jax import lax
@@ -31,217 +29,32 @@
     return lax.broadcasted_iota(jnp.int32, shape, 1)
 
 
-def scan_kernel(
-    n_ctx,
-    blocks,
-    proj,
-    bc,
-    decay,
-    taps,
-    gain,
-    out,
-    cum,
-    inner,
-    starts,
-    offsets,
-    within,
-    halo,
-    mine,
-    carries,
-    halo_sems,
-    send_sems,
-    recv_sems,
-):
-    me = lax.axis_index("ctx")
-    barrier = pltpu.get_barrier_semaphore()
-    for r in range(1, n_ctx):
-        pl.semaphore_signal(
-            barrier,
-            inc=1,
-            device_id={"ctx": lax.rem(me + r, n_ctx)},
-            device_id_type=MESH,
-        )
-
-    upper = (
-        lax.broadcasted_iota(jnp.int32, (Q, Q), 0)
-        <= lax.broadcasted_iota(jnp.int32, (Q, Q), 1)
-    ).astype(BF16)
-    steps = decay[...].reshape(blocks * 8, Q)
-    high, rest = split2(steps)
-    lowest = (steps - high.astype(F32) - rest.astype(F32)).astype(BF16)
-    total = jnp.dot(lowest, upper, preferred_element_type=F32)
-    total = total + jnp.dot(rest, upper, preferred_element_type=F32)
-    total = total + jnp.dot(high, upper, preferred_element_type=F32)
-    cum[...] = total.reshape(blocks, 8, Q)
-
-    pl.semaphore_wait(barrier, n_ctx - 1)
-    rows = blocks * Q
-    halo_copy = pltpu.make_async_remote_copy(
-        src_ref=proj.at[pl.ds(rows - HALO, HALO)],
-        dst_ref=halo,
-        send_sem=halo_sems.at[0],
-        recv_sem=halo_sems.at[1],
-        device_id={"ctx": lax.rem(me + 1, n_ctx)},
-        device_id_type=MESH,
-    )
-    halo_copy.start()
-    halo_copy.wait()
-
-    def by_position(block):
-        rows_of = cum[block]
-        both = jnp.concatenate(
-            [
-                jnp.broadcast_to(rows_of[h : h + 1], (P_SIZE, Q))
-                for h in range(2)
-            ],
-            axis=0,
-        )
-        return both.T
-
-    def states(block, carry):
-        tail, state, offset = carry
-        base = pl.multiple_of(block * Q, Q)
-        current = proj[pl.ds(base, Q), :].astype(F32)
-        window = jnp.concatenate([tail, current], axis=0)
-        summed = taps[0:1] * window[5 : 5 + Q]
-        for k in range(1, 4):
-            summed = summed + taps[k : k + 1] * window[5 + k : 5 + k + Q]
-        own = jax.nn.silu(summed).astype(BF16)
-        inner[pl.ds(base, Q), :] = own
-        positions = by_position(block)
-        last = positions[Q - 1 : Q]
-        scaled = (own.astype(F32) * jnp.exp(last - positions)).astype(BF16)
-        b_part = bc[pl.ds(base, Q), :N]
-        added = lax.dot_general(b_part, scaled, TN, preferred_element_type=F32)
-        starts[block] = state
-        offsets[block] = jnp.broadcast_to(offset, (8, N))
-        return current[Q - 8 :], jnp.exp(last) * state + added, offset + last
-
-    first = jnp.where(me == 0, 0.0, halo[...].astype(F32))[HALO - 8 :]
-    _, state, offset = lax.fori_loop(
-        0,
-        blocks,
-        states,
-        (first, jnp.zeros((N, 2 * P_SIZE), F32), jnp.zeros((1, 2 * P_SIZE), F32)),
-        unroll=4,
-    )
-    mine[0:N] = state
-    mine[N : N + 8] = jnp.broadcast_to(jnp.exp(offset), (8, 2 * P_SIZE))
-
-    def carry_copy(r):
-        return pltpu.make_async_remote_copy(
-            src_ref=mine,
-            dst_ref=carries.at[r - 1],
-            send_sem=send_sems.at[r - 1],
-            recv_sem=recv_sems.at[r - 1],
-            device_id={"ctx": lax.rem(me + r, n_ctx)},
-            device_id_type=MESH,
-        )
-
-    for r in range(1, n_ctx):
-        carry_copy(r).start()
-
-    mask = lax.broadcasted_iota(jnp.int32, (Q, Q), 0) >= lax.broadcasted_iota(
-        jnp.int32, (Q, Q), 1
-    )
-    first_head = lane_of((Q, 2 * P_SIZE)) < P_SIZE
-
-    def inside(block, _):
-        base = pl.multiple_of(block * Q, Q)
-        b_part = bc[pl.ds(base, Q), :N]
-        c_part = bc[pl.ds(base, Q), N:]
-        own = inner[pl.ds(base, Q), :]
-        scores = lax.dot_general(c_part, b_part, NT, preferred_element_type=F32)
-        rows_of = cum[block]
-        parts = []
-        for h in range(2):
-            along = rows_of[h : h + 1]
-            down = jnp.broadcast_to(along, (2 * P_SIZE, Q)).T
-            down = jnp.concatenate([down, down], axis=1)
-            weights = jnp.exp(jnp.where(mask, down - along, -1e30))
-            weighted = (scores * weights).astype(BF16)
-            parts.append(jnp.dot(weighted, own, preferred_element_type=F32))
-        within[pl.ds(base, Q), :] = jnp.where(first_head, parts[0], parts[1])
-        return 0
-
-    lax.fori_loop(0, blocks, inside, 0, unroll=4)
-
-    for r in range(1, n_ctx):
-        carry_copy(r).wait()
-    carried = jnp.zeros((N, 2 * P_SIZE), F32)
-    for r in range(n_ctx - 1, 0, -1):
-        new = carries[r - 1, N : N + 1] * carried + carries[r - 1, 0:N]
-        carried = jnp.where(me - r >= 0, new, carried)
-
-    same_head = (
-        lax.broadcasted_iota(jnp.int32, (2 * N, 2 * P_SIZE), 0) % (2 * P_SIZE)
-        // P_SIZE
-        == lane_of((2 * N, 2 * P_SIZE)) // P_SIZE
-    )
-    averaging = jnp.where(same_head, 1.0 / P_SIZE, 0.0).astype(BF16)
-
-    def finish(block, _):
-        base = pl.multiple_of(block * Q, Q)
-        c_part = bc[pl.ds(base, Q), N:]
-        state = starts[block] + jnp.exp(offsets[block, 0:1]) * carried
-        from_state = jnp.dot(
-            jnp.concatenate([c_part, c_part], axis=1),
-            jnp.concatenate(split2(state), axis=0),
-            preferred_element_type=F32,
-        )
-        value = within[pl.ds(base, Q), :] + jnp.exp(by_position(block)) * from_state
-        squares = jnp.concatenate(split2(value * value), axis=1)
-        mean = jnp.dot(squares, averaging, preferred_element_type=F32)
-        normed = value * lax.rsqrt(mean + epsilon) * gain[0:1]
-        out[pl.ds(base, Q), :] = normed.astype(BF16)
-        return 0
-
-    lax.fori_loop(0, blocks, finish, 0, unroll=4)
-
-
-def scan(n_ctx, proj, bc, decay, taps, gain):
-    rows = proj.shape[0]
-    blocks = rows // Q
-    width = 2 * P_SIZE
-    vmem = pl.BlockSpec(memory_space=pltpu.VMEM)
-    return pl.pallas_call(
-        functools.partial(scan_kernel, n_ctx, blocks),
-        out_shape=jax.ShapeDtypeStruct((rows, width), BF16),
-        in_specs=[vmem] * 5,
-        out_specs=vmem,
-        scratch_shapes=[
-            pltpu.VMEM((blocks, 8, Q), F32),
-            pltpu.VMEM((rows, width), BF16),
-            pltpu.VMEM((blocks, N, width), F32),
-            pltpu.VMEM((blocks, 8, width), F32),
-            pltpu.VMEM((rows, width), F32),
-            pltpu.VMEM((HALO, width), BF16),
-            pltpu.VMEM((N + 8, width), F32),
-            pltpu.VMEM((n_ctx - 1, N + 8, width), F32),
-            pltpu.SemaphoreType.DMA((2,)),
-            pltpu.SemaphoreType.DMA((n_ctx - 1,)),
-            pltpu.SemaphoreType.DMA((n_ctx - 1,)),
-        ],
-        compiler_params=pltpu.CompilerParams(
-            collective_id=1, has_side_effects=True, vmem_limit_bytes=48 * 2**20
-        ),
-    )(proj, bc, decay, taps, gain)
-
-
 NX, NY, NZ = 4, 4, 8
 ROWS = 256
 DEPTH = 2560
 SHARD = 80
-HEAD_COLUMNS = 1024
+BLOCKS = NY * NZ
+WIDTH = 2 * P_SIZE
 STATE_AT = 4096
 
 
-def exchange_kernel(
+def layer_kernel(
     tokens,
     w_in,
-    taps,
+    conv,
+    decay,
+    gain,
+    out,
     proj,
     bc,
+    cum,
+    inner,
+    starts,
+    lasts,
+    offsets,
+    within,
+    mine,
+    carries,
     tok,
     weights,
     state_weights,
@@ -262,6 +75,9 @@
     bc_recv,
     out_send,
     out_recv,
+    edge_sems,
+    carry_send,
+    carry_recv,
 ):
     ctx = lax.axis_index("ctx")
     f = lax.axis_index("fsdp")
@@ -296,6 +112,9 @@
     def block(index):
         return pl.ds(pl.multiple_of(index * Q, Q), Q)
 
+    def positions(index):
+        return pl.ds(pl.multiple_of(index * Q + HALO, HALO), Q)
+
     half = columns(c)
     other_half = columns(1 - c)
     devices = NY * NZ
@@ -310,9 +129,8 @@
         return 0
 
     lax.fori_loop(1, devices, greet_row, 0)
-    for dx in range(1, NX):
-        greet(at(dx=dx))
-    greet(at(dc=1))
+    for r in range(1, 2 * NX):
+        greet({"ctx": lax.rem(ctx + r, 2 * NX), "fsdp": f})
     greet(
         {
             "ctx": lax.rem(ctx + 2 * NX - (devices - f) // devices, 2 * NX),
@@ -339,7 +157,7 @@
     def _():
         own_state_shard.start()
 
-    pl.semaphore_wait(barrier, devices - 1 + NX - 1 + 2)
+    pl.semaphore_wait(barrier, devices - 1 + 2 * NX - 1 + 1)
 
     def give_shard(r, _):
         other = lax.rem(f + r, devices)
@@ -399,6 +217,21 @@
     tok_copy(0, 1, 3, 1).start()
     tok_copy(0, 1, 1, 3).start()
     tok_copy(0, 0, 3, 1).start()
+
+    upper = (
+        lax.broadcasted_iota(jnp.int32, (Q, Q), 0)
+        <= lax.broadcasted_iota(jnp.int32, (Q, Q), 1)
+    ).astype(BF16)
+    for index in range(BLOCKS):
+        pair = decay[:, index * Q : (index + 1) * Q]
+        cum[index] = jnp.concatenate([pair] * 4, axis=0)
+    steps = cum[...].reshape(BLOCKS * 8, Q)
+    high, rest = split2(steps)
+    lowest = (steps - high.astype(F32) - rest.astype(F32)).astype(BF16)
+    total = jnp.dot(lowest, upper, preferred_element_type=F32)
+    total = total + jnp.dot(rest, upper, preferred_element_type=F32)
+    total = total + jnp.dot(high, upper, preferred_element_type=F32)
+    cum[...] = total.reshape(BLOCKS, 8, Q)
 
     def tok_arrived(slot, part):
         settle(tok.at[slot, pl.ds(part * (ROWS // 2), ROWS // 2)], tok_recv.at[slot, part])
@@ -464,7 +297,7 @@
 
     def out_piece(t, s, side):
         away = lax.rem(2 * lax.rem(x + s, NX) + side, NZ)
-        rows = block(lax.rem(y + t, NY) * NZ + z)
+        rows = positions(lax.rem(y + t, NY) * NZ + z)
         return pieces.at[t, s, :, pl.ds(side * 128, 128)], rows, away
 
     def multiply(t, s):
@@ -531,9 +364,9 @@
     window = jnp.concatenate(
         [before[HALO - 8 :], here.astype(BF16).astype(F32)], axis=0
     )
-    summed = taps[0:1] * window[5 : 5 + ROWS]
+    summed = conv[0:1, STATE_AT:] * window[5 : 5 + ROWS]
     for k in range(1, 4):
-        summed = summed + taps[k : k + 1] * window[5 + k : 5 + k + ROWS]
+        summed = summed + conv[k : k + 1, STATE_AT:] * window[5 + k : 5 + k + ROWS]
     bc[block(f), :] = jax.nn.silu(summed).astype(BF16)
 
     ring_copy(0, 0).start()
@@ -605,21 +438,189 @@
     multiply(2, 1)
     multiply(2, 2)
 
-    for k in (0, 7, 1, 6, 2, 5, 3, 4):
+    def heads_arrived(t):
+        rows = lax.rem(y + t, NY) * NZ
+        settle(proj.at[positions(rows + z)], out_send.at[0, t])
+        for away in range(1, NZ):
+            source = lax.rem(z + NZ - away, NZ)
+            settle(proj.at[positions(rows + source)], out_recv.at[away, t])
+
+    edge = remote(
+        proj.at[pl.ds(BLOCKS * Q, HALO)],
+        proj.at[pl.ds(0, HALO)],
+        edge_sems.at[0],
+        edge_sems.at[1],
+        {"ctx": lax.rem(ctx + 1, 2 * NX), "fsdp": f},
+    )
+
+    def by_position(index):
+        rows_of = cum[index]
+        both = jnp.concatenate(
+            [jnp.broadcast_to(rows_of[h : h + 1], (P_SIZE, Q)) for h in range(2)],
+            axis=0,
+        )
+        return both.T
+
+    def place(i):
+        return lax.rem(y + i // NZ, NY) * NZ + lax.rem(i, NZ)
+
+    mine_taps = columns(f)
+
+    def convolve(i, _):
+        index = place(i)
+        base = pl.multiple_of(index * Q, Q)
+        above = proj[pl.ds(base, HALO), :].astype(F32)[HALO - 8 :]
+        above = jnp.where(ctx + index == 0, 0.0, above)
+        current = proj[positions(index), :].astype(F32)
+        window = jnp.concatenate([above, current], axis=0)
+        summed = conv[0:1, mine_taps] * window[5 : 5 + Q]
+        for k in range(1, 4):
+            summed = summed + conv[k : k + 1, mine_taps] * window[5 + k : 5 + k + Q]
+        own = jax.nn.silu(summed).astype(BF16)
+        inner[pl.ds(base, Q), :] = own
+        decays = by_position(index)
+        last = decays[Q - 1 : Q]
+        scaled = (own.astype(F32) * jnp.exp(last - decays)).astype(BF16)
+        b_part = bc[pl.ds(base, Q), :N]
+        starts[index] = lax.dot_general(b_part, scaled, TN, preferred_element_type=F32)
+        lasts[index] = jnp.broadcast_to(last, (8, WIDTH))
+        return 0
+
+    mask = lax.broadcasted_iota(jnp.int32, (Q, Q), 0) >= lax.broadcasted_iota(
+        jnp.int32, (Q, Q), 1
+    )
+    first_head = lane_of((Q, WIDTH)) < P_SIZE
+
+    def inside(i, _):
+        index = place(i)
+        base = pl.multiple_of(index * Q, Q)
+        b_part = bc[pl.ds(base, Q), :N]
+        c_part = bc[pl.ds(base, Q), N:]
+        own = inner[pl.ds(base, Q), :]
+        scores = lax.dot_general(c_part, b_part, NT, preferred_element_type=F32)
+        rows_of = cum[index]
+        parts = []
+        for h in range(2):
+            along = rows_of[h : h + 1]
+            down = jnp.broadcast_to(along, (WIDTH, Q)).T
+            down = jnp.concatenate([down, down], axis=1)
+            factors = jnp.exp(jnp.where(mask, down - along, -1e30))
+            weighted = (scores * factors).astype(BF16)
+            parts.append(jnp.dot(weighted, own, preferred_element_type=F32))
+        within[pl.ds(base, Q), :] = jnp.where(first_head, parts[0], parts[1])
+        return 0
+
+    def bc_forward(k):
         settle(bc.at[block(bc_rows(3, k))], bc_recv.at[3, k, 0])
         bc_copy(3, k, 0).start()
         settle(bc.at[block(bc_rows(1, k))], bc_recv.at[1, k, 0])
         bc_copy(1, k, 1).start()
 
+    for k in (0, 7, 1, 6, 2, 5, 3, 4):
+        bc_forward(k)
+
+    for t in (0, 3, 1):
+        heads_arrived(t)
+
+    @pl.when(y != 1)
+    def _():
+        edge.start()
+
+    @pl.when(jnp.logical_or(y == 0, y == 3))
+    def _():
+        edge.wait_recv()
+
+    lax.fori_loop(0, 2 * NZ, convolve, 0, unroll=4)
+    lax.fori_loop(0, 2 * NZ, inside, 0, unroll=4)
+
+    heads_arrived(2)
+
+    @pl.when(y == 1)
+    def _():
+        edge.start()
+
+    for k in range(8):
+        index = bc_rows(2, k)
+        for way in range(2):
+            settle(
+                bc.at[pl.ds(pl.multiple_of(index * Q + way * (Q // 2), Q // 2), Q // 2)],
+                bc_recv.at[2, k, way],
+            )
+
+    @pl.when(jnp.logical_or(y == 1, y == 2))
+    def _():
+        edge.wait_recv()
+
+    lax.fori_loop(2 * NZ, 4 * NZ, convolve, 0, unroll=4)
+
+    def follow(index, carry):
+        state, offset = carry
+        added = starts[index]
+        last = lasts[index, 0:1]
+        starts[index] = state
+        offsets[index] = jnp.broadcast_to(offset, (8, WIDTH))
+        return jnp.exp(last) * state + added, offset + last
+
+    state, offset = lax.fori_loop(
+        0,
+        BLOCKS,
+        follow,
+        (jnp.zeros((N, WIDTH), F32), jnp.zeros((1, WIDTH), F32)),
+        unroll=2,
+    )
+    mine[0:N] = state
+    mine[N : N + 8] = jnp.broadcast_to(jnp.exp(offset), (8, WIDTH))
+
+    def carry_copy(r):
+        return remote(
+            mine,
+            carries.at[r - 1],
+            carry_send.at[r - 1],
+            carry_recv.at[r - 1],
+            {"ctx": lax.rem(ctx + r, 2 * NX), "fsdp": f},
+        )
+
+    for r in range(1, 2 * NX):
+        carry_copy(r).start()
+    lax.fori_loop(2 * NZ, 4 * NZ, inside, 0, unroll=4)
+    for r in range(1, 2 * NX):
+        carry_copy(r).wait_recv()
+    carried = jnp.zeros((N, WIDTH), F32)
+    for r in range(2 * NX - 1, 0, -1):
+        new = carries[r - 1, N : N + 1] * carried + carries[r - 1, 0:N]
+        carried = jnp.where(ctx - r >= 0, new, carried)
+
+    same_head = (
+        lax.broadcasted_iota(jnp.int32, (2 * N, WIDTH), 0) % WIDTH // P_SIZE
+        == lane_of((2 * N, WIDTH)) // P_SIZE
+    )
+    averaging = jnp.where(same_head, 1.0 / P_SIZE, 0.0).astype(BF16)
+
+    def finish(index, _):
+        base = pl.multiple_of(index * Q, Q)
+        c_part = bc[pl.ds(base, Q), N:]
+        start = starts[index] + jnp.exp(offsets[index, 0:1]) * carried
+        from_state = jnp.dot(
+            jnp.concatenate([c_part, c_part], axis=1),
+            jnp.concatenate(split2(start), axis=0),
+            preferred_element_type=F32,
+        )
+        value = within[pl.ds(base, Q), :] + jnp.exp(by_position(index)) * from_state
+        squares = jnp.concatenate(split2(value * value), axis=1)
+        mean = jnp.dot(squares, averaging, preferred_element_type=F32)
+        normed = value * lax.rsqrt(mean + epsilon) * gain[0:1]
+        out[pl.ds(base, Q), :] = normed.astype(BF16)
+        return 0
+
+    lax.fori_loop(0, BLOCKS, finish, 0, unroll=4)
+
+    edge.wait_send()
+    for r in range(1, 2 * NX):
+        carry_copy(r).wait_send()
     for k in range(8):
         for way in range(2):
             bc_copy(0, k, way).wait_send()
             bc_copy(3 if way == 0 else 1, k, way).wait_send()
-            index = bc_rows(2, k)
-            settle(
-                bc.at[pl.ds(pl.multiple_of(index * Q + way * (Q // 2), Q // 2), Q // 2)],
-                bc_recv.at[2, k, way],
-            )
     for k, way in ((0, 0), (0, 1), (7, 0), (1, 1), (6, 0), (2, 1), (5, 0)):
         ring_copy(k, way).wait_send()
     for slot in range(4):
@@ -645,27 +646,31 @@
         )
 
     for t in range(NY):
-        rows = lax.rem(y + t, NY) * NZ
-        settle(proj.at[block(rows + z)], out_send.at[0, t])
         for away in range(1, NZ):
-            settle(proj.at[block(rows + z)], out_send.at[away, t])
-            source = lax.rem(z + NZ - away, NZ)
-            settle(proj.at[block(rows + source)], out_recv.at[away, t])
-
-
-def exchange(tokens, w_in, taps):
+            settle(proj.at[positions(0)], out_send.at[away, t])
+
+
+def layer(tokens, w_in, conv_weight, steps, gain):
     vmem = pl.BlockSpec(memory_space=pltpu.VMEM)
+    hbm = pl.BlockSpec(memory_space=pl.ANY)
     dma = pltpu.SemaphoreType.DMA
-    blocks = NY * NZ
+    rows = BLOCKS * Q
     return pl.pallas_call(
-        exchange_kernel,
-        out_shape=[
-            jax.ShapeDtypeStruct((blocks * Q, 2 * P_SIZE), BF16),
-            jax.ShapeDtypeStruct((blocks * Q, 2 * N), BF16),
-        ],
-        in_specs=[vmem] * 3,
-        out_specs=[vmem] * 2,
+        layer_kernel,
+        out_shape=jax.ShapeDtypeStruct((rows, WIDTH), BF16),
+        in_specs=[hbm] * 2 + [vmem] * 3,
+        out_specs=vmem,
         scratch_shapes=[
+            pltpu.VMEM((HALO + rows, WIDTH), BF16),
+            pltpu.VMEM((rows, 2 * N), BF16),
+            pltpu.VMEM((BLOCKS, 8, Q), F32),
+            pltpu.VMEM((rows, WIDTH), BF16),
+            pltpu.VMEM((BLOCKS, N, WIDTH), F32),
+            pltpu.VMEM((BLOCKS, 8, WIDTH), F32),
+            pltpu.VMEM((BLOCKS, 8, WIDTH), F32),
+            pltpu.VMEM((rows, WIDTH), F32),
+            pltpu.VMEM((N + 8, WIDTH), F32),
+            pltpu.VMEM((2 * NX - 1, N + 8, WIDTH), F32),
             pltpu.VMEM((NY, ROWS, DEPTH), BF16),
             pltpu.VMEM((NX, DEPTH, 256), BF16),
             pltpu.VMEM((DEPTH, 2 * N), BF16),
@@ -686,30 +691,18 @@
             dma((4, 8, 2)),
             dma((8, 4)),
             dma((8, 4)),
+            dma((2,)),
+            dma((2 * NX - 1,)),
+            dma((2 * NX - 1,)),
         ],
         compiler_params=pltpu.CompilerParams(
-            collective_id=2, has_side_effects=True, vmem_limit_bytes=48 * 2**20
+            collective_id=3, has_side_effects=True, vmem_limit_bytes=56 * 2**20
         ),
-    )(tokens, w_in, taps)
-
-
-def scan_operands(log_decay, conv_weight, norm_gain):
-    rows = log_decay.shape[0]
-    blocks = rows // Q
-    steps = log_decay.T.reshape(2, blocks, Q).transpose(1, 0, 2)
-    steps = jnp.pad(steps, ((0, 0), (0, 6), (0, 0)))
-    width = 2 * P_SIZE
-    mine = lax.dynamic_slice_in_dim(
-        conv_weight, lax.axis_index("fsdp") * width, width, axis=1
-    )
-    return steps, jnp.pad(mine, ((0, 4), (0, 0))), jnp.broadcast_to(norm_gain, (8, width))
+    )(tokens, w_in, conv_weight, steps, gain)
 
 
 def body(tokens, w_in, conv_weight, log_decay, norm_gain):
-    state_taps = jnp.pad(conv_weight[:, STATE_AT:], ((0, 4), (0, 0)))
-    heads, state_rows = exchange(tokens, w_in, state_taps)
-    steps, taps, gain = scan_operands(log_decay, conv_weight, norm_gain)
-    return scan(lax.axis_size("ctx"), heads, state_rows, steps, taps, gain)
+    return layer(tokens, w_in, conv_weight, log_decay.T, norm_gain.reshape(1, WIDTH))
 
 
 def solution(mesh):

time: 149 us -> 139 us (0.933)
  Pallas kernels: 142 us -> 136 us
  local copies, waits for them, and re-layouts: 6.63 us -> 3.05 us
    pallas_call x2 -> x1, Pallas kernels: 142 us -> 136 us  [layer(): pl.pallas_call(layer_kernel, out_shape=jax.ShapeDtypeStruct((rows, WIDTH)...]
    unnamed x5 -> x1, local copies, waits for them, and re-layouts: 3.73 us -> 3.05 us
where the time goes in v4:
time: 139 us
  Pallas kernels  136 us (98%)
  local copies, waits for them, and re-layouts  3.05 us (2%)
    pallas_call x1, Pallas kernels, layer(): pl.pallas_call(layer_kernel, out_shape=jax.ShapeDtypeStruct((rows, WIDTH)...  136 us
    unnamed x1, local copies, waits for them, and re-layouts  3.05 us

profile of v4, /device:TPU:1, one launch (start us, length us, event | category | flops | bytes accessed | tf_op | source)
XLA Modules:
  0.0 138.8 jit_solution(9755795308333268394)
XLA Ops:
  0.0 135.7 %shard_map.55 = bf16[8192,128]{1,0:T(8,128)(2,1)} custom-call(bf16[256,2560]{1,0:T(8,128)(2,1)} %tokens.1, bf16[80,4352]{1,0:T(8,128)(2,1)} %w_in.1, f32[4,4352]{1,0:T(4,128)} %conv.1, f32[2,8192]{1,0:T(2,128)} %bitcast.2, f32[1,128]{1,0:T(1,128)} %bitcast.3), custom_call_target="tpu_custom_call" | custom-call | tf_op jit(solution)/shard_map/pallas_call | solution.py:658
  135.7 3.0 %copy.7 = bf16[8192,128]{1,0:T(8,128)(2,1)} copy(bf16[8192,128]{1,0:T(8,128)(2,1)} %shard_map.55) | data formatting | bytes 4194304

commit v5 on v4

--- a/solution.py
+++ b/solution.py
@@ -259,14 +259,18 @@
     def bc_rows(t, k):
         return lax.rem(y + t, NY) * NZ + lax.rem(z + k, NZ)
 
-    def ring_copy(k, way):
-        rows = bc.at[block(bc_rows(0, k))]
+    def ring_rows(k, part):
+        at_row = bc_rows(0, k) * Q + part * (Q // 2)
+        return bc.at[pl.ds(pl.multiple_of(at_row, Q // 2), Q // 2)]
+
+    def ring_part(k, way, part):
+        rows = ring_rows(k, part)
         target = (k + 7) % 8 if way == 0 else k + 1
         return remote(
             rows,
             rows,
-            ring_send.at[k, way],
-            ring_recv.at[target],
+            ring_send.at[k, way, part],
+            ring_recv.at[target, part],
             at(dz=1 if way == 0 else NZ - 1),
         )
 
@@ -288,8 +292,8 @@
             at(dy=1 if way == 0 else NY - 1),
         )
 
-    def ring_arrived(k):
-        settle(bc.at[block(bc_rows(0, k))], ring_recv.at[k])
+    def ring_arrived(k, part):
+        settle(ring_rows(k, part), ring_recv.at[k, part])
 
     def bc_on(k):
         bc_copy(0, k, 0).start()
@@ -369,8 +373,9 @@
         summed = summed + conv[k : k + 1, STATE_AT:] * window[5 + k : 5 + k + ROWS]
     bc[block(f), :] = jax.nn.silu(summed).astype(BF16)
 
-    ring_copy(0, 0).start()
-    ring_copy(0, 1).start()
+    for part in range(2):
+        ring_part(0, 0, part).start()
+        ring_part(0, 1, part).start()
     own_shard.wait()
     settle(
         weights.at[0, pl.ds(0, (devices - 1) * SHARD), half], shard_sems.at[1]
@@ -384,27 +389,31 @@
     tok_arrived(1, 1)
     tok_copy(1, 1, 3, 2).start()
 
-    ring_arrived(7)
-    ring_copy(7, 0).start()
-    ring_arrived(1)
-    ring_copy(1, 1).start()
+    for part in range(2):
+        ring_arrived(7, part)
+        ring_part(7, 0, part).start()
+        ring_arrived(1, part)
+        ring_part(1, 1, part).start()
     core_arrived(0)
     multiply(0, 0)
     bc_on(0)
     bc_on(7)
     bc_on(1)
-    ring_arrived(6)
-    ring_copy(6, 0).start()
-    ring_arrived(2)
-    ring_copy(2, 1).start()
+    for part in range(2):
+        ring_arrived(6, part)
+        ring_part(6, 0, part).start()
+        ring_arrived(2, part)
+        ring_part(2, 1, part).start()
     bc_on(6)
     bc_on(2)
-    ring_arrived(5)
-    ring_copy(5, 0).start()
-    ring_arrived(3)
+    for part in range(2):
+        ring_arrived(5, part)
+        ring_part(5, 0, part).start()
+        ring_arrived(3, part)
     bc_on(5)
     bc_on(3)
-    ring_arrived(4)
+    ring_arrived(4, 0)
+    ring_arrived(4, 1)
     bc_on(4)
     tok_arrived(3, 1)
     multiply(3, 0)
@@ -539,6 +548,12 @@
     def _():
         edge.start()
 
+    @pl.when(jnp.logical_or(y == 1, y == 2))
+    def _():
+        edge.wait_recv()
+
+    lax.fori_loop(3 * NZ, 4 * NZ, convolve, 0, unroll=4)
+    lax.fori_loop(3 * NZ, 4 * NZ, inside, 0, unroll=4)
     for k in range(8):
         index = bc_rows(2, k)
         for way in range(2):
@@ -547,11 +562,7 @@
                 bc_recv.at[2, k, way],
             )
 
-    @pl.when(jnp.logical_or(y == 1, y == 2))
-    def _():
-        edge.wait_recv()
-
-    lax.fori_loop(2 * NZ, 4 * NZ, convolve, 0, unroll=4)
+    lax.fori_loop(2 * NZ, 3 * NZ, convolve, 0, unroll=8)
 
     def follow(index, carry):
         state, offset = carry
@@ -568,8 +579,11 @@
         (jnp.zeros((N, WIDTH), F32), jnp.zeros((1, WIDTH), F32)),
         unroll=2,
     )
-    mine[0:N] = state
-    mine[N : N + 8] = jnp.broadcast_to(jnp.exp(offset), (8, WIDTH))
+    mine[0:N] = state.astype(BF16)
+    fall = split2(jnp.exp(offset))
+    mine[N : N + HALO] = jnp.concatenate(
+        [jnp.broadcast_to(part, (HALO // 2, WIDTH)) for part in fall], axis=0
+    )
 
     def carry_copy(r):
         return remote(
@@ -582,12 +596,14 @@
 
     for r in range(1, 2 * NX):
         carry_copy(r).start()
-    lax.fori_loop(2 * NZ, 4 * NZ, inside, 0, unroll=4)
+    lax.fori_loop(2 * NZ, 3 * NZ, inside, 0, unroll=4)
     for r in range(1, 2 * NX):
         carry_copy(r).wait_recv()
     carried = jnp.zeros((N, WIDTH), F32)
     for r in range(2 * NX - 1, 0, -1):
-        new = carries[r - 1, N : N + 1] * carried + carries[r - 1, 0:N]
+        fall = carries[r - 1, N : N + HALO].astype(F32)
+        fall = fall[0:1] + fall[HALO // 2 : HALO // 2 + 1]
+        new = fall * carried + carries[r - 1, 0:N].astype(F32)
         carried = jnp.where(ctx - r >= 0, new, carried)
 
     same_head = (
@@ -609,10 +625,14 @@
         squares = jnp.concatenate(split2(value * value), axis=1)
         mean = jnp.dot(squares, averaging, preferred_element_type=F32)
         normed = value * lax.rsqrt(mean + epsilon) * gain[0:1]
-        out[pl.ds(base, Q), :] = normed.astype(BF16)
+        inner[pl.ds(base, Q), :] = normed.astype(BF16)
+        pltpu.make_async_copy(
+            inner.at[pl.ds(base, Q)], out.at[pl.ds(base, Q)], own_sems.at[3]
+        ).start()
         return 0
 
-    lax.fori_loop(0, BLOCKS, finish, 0, unroll=4)
+    lax.fori_loop(0, BLOCKS, finish, 0, unroll=8)
+    settle(inner, own_sems.at[3])
 
     edge.wait_send()
     for r in range(1, 2 * NX):
@@ -622,7 +642,8 @@
             bc_copy(0, k, way).wait_send()
             bc_copy(3 if way == 0 else 1, k, way).wait_send()
     for k, way in ((0, 0), (0, 1), (7, 0), (1, 1), (6, 0), (2, 1), (5, 0)):
-        ring_copy(k, way).wait_send()
+        ring_part(k, way, 0).wait_send()
+        ring_part(k, way, 1).wait_send()
     for slot in range(4):
         core_copy(slot).wait_send()
     state_core.wait_send()
@@ -659,7 +680,7 @@
         layer_kernel,
         out_shape=jax.ShapeDtypeStruct((rows, WIDTH), BF16),
         in_specs=[hbm] * 2 + [vmem] * 3,
-        out_specs=vmem,
+        out_specs=hbm,
         scratch_shapes=[
             pltpu.VMEM((HALO + rows, WIDTH), BF16),
             pltpu.VMEM((rows, 2 * N), BF16),
@@ -669,14 +690,14 @@
             pltpu.VMEM((BLOCKS, 8, WIDTH), F32),
             pltpu.VMEM((BLOCKS, 8, WIDTH), F32),
             pltpu.VMEM((rows, WIDTH), F32),
-            pltpu.VMEM((N + 8, WIDTH), F32),
-            pltpu.VMEM((2 * NX - 1, N + 8, WIDTH), F32),
+            pltpu.VMEM((N + HALO, WIDTH), BF16),
+            pltpu.VMEM((2 * NX - 1, N + HALO, WIDTH), BF16),
             pltpu.VMEM((NY, ROWS, DEPTH), BF16),
             pltpu.VMEM((NX, DEPTH, 256), BF16),
             pltpu.VMEM((DEPTH, 2 * N), BF16),
             pltpu.VMEM((NY, NX, ROWS, 256), BF16),
             pltpu.VMEM((HALO, DEPTH), BF16),
-            dma((3,)),
+            dma((4,)),
             dma((2,)),
             dma((4, 2, 2)),
             dma((4, 2)),
@@ -685,8 +706,8 @@
             dma((4, 2)),
             dma((5,)),
             dma((5,)),
+            dma((8, 2, 2)),
             dma((8, 2)),
-            dma((8,)),
             dma((4, 8, 2)),
             dma((4, 8, 2)),
             dma((8, 4)),

time: 139 us -> 134 us (0.964)
  Pallas kernels: 136 us -> 131 us
    pallas_call x1, Pallas kernels: 136 us -> 131 us  [layer(): pl.pallas_call(layer_kernel, out_shape=jax.ShapeDtypeStruct((rows, WIDTH)...]
where the time goes in v5:
time: 134 us
  Pallas kernels  131 us (98%)
  local copies, waits for them, and re-layouts  3.05 us (2%)
    pallas_call x1, Pallas kernels, layer(): pl.pallas_call(layer_kernel, out_shape=jax.ShapeDtypeStruct((rows, WIDTH)...  131 us
    unnamed x1, local copies, waits for them, and re-layouts  3.05 us

profile of v5, /device:TPU:1, one launch (start us, length us, event | category | flops | bytes accessed | tf_op | source)
XLA Modules:
  0.0 134.0 jit_solution(15830944226051601175)
XLA Ops:
  0.0 131.0 %shard_map.55 = bf16[8192,128]{1,0:T(8,128)(2,1)} custom-call(bf16[256,2560]{1,0:T(8,128)(2,1)} %tokens.1, bf16[80,4352]{1,0:T(8,128)(2,1)} %w_in.1, f32[4,4352]{1,0:T(4,128)} %conv.1, f32[2,8192]{1,0:T(2,128)} %bitcast.2, f32[1,128]{1,0:T(1,128)} %bitcast.3), custom_call_target="tpu_custom_call" | custom-call | tf_op jit(solution)/shard_map/pallas_call | solution.py:679
  131.0 3.0 %copy.7 = bf16[8192,128]{1,0:T(8,128)(2,1)} copy(bf16[8192,128]{1,0:T(8,128)(2,1)} %shard_map.55) | data formatting | bytes 4194304
